TPU v7x, 32 devices: a whole 2x2x4 slice. The times are simulated.
32 devices in a mesh: study: 16 (over z, y, x), cell: 2 (over core).
Axes of the slice: x: 2, y: 2, z: 4, core: 2. Of those that a mesh axis runs over, the one named last changes fastest.
Arguments:
- latents: bfloat16 [16, 1024, 64], P('study', 'cell'), may hold values from -8 to 8
- donor_ids: int32 [16, 1024], P('study', 'cell'), may hold values from 0 to 15, as said below
- study_valid_length: int32 [16], P('study'), may hold values from 1 to 1024, 12288 in all
- study_penalty_weight: float32 [16], P('study'), may hold values from 1 to 8
- frequencies: bfloat16 [64, 8192], replicated, may hold values from -0.75 to 0.75
- phases: float32 [8192], replicated, may hold values from -3.140625 to 3.140625
Outputs:
- latent_grad: float32 [16, 1024, 64], P('study', 'cell')
Inputs may be any that keep to these rules, and one draw needn't show every extreme that they name: `donor_ids`: donor ids never fall along a study's window; every study's window begins with donor 0 and ends with donor 16 - 1.
All inputs are finite; a program needn't handle non-finite values. No bound on the sum of `study_valid_length` on one device may be relied on, other than what follows from the above.
Results may differ from a plain program's by a relative error of at most 0.00045.
Values may be sent and summed in bfloat16 or wider, within the bound.
No kernel may reach another device: no remote copies, remote signals or barrier semaphores. Data moves between devices by JAX's collectives and lax.ppermute only.
A program may use at most 64 MiB of HBM per device.

v0:
```python
import functools
import math

import jax
import jax.numpy as jnp
from jax import lax
from jax.experimental import pallas as pl
from jax.experimental.pallas import tpu as pltpu
from jax.sharding import PartitionSpec as P

DONOR_LABELS = 16
FEATURE_PENALTY = 16.0
BLOCK = 256
DEPTH = 256
SUBLANES = 8
MIB = 1 << 20

COS_LEAD = -0.552051508388134
COS_TERMS = (-4.602194203577409, 9.359560663732573, -5.6907268683441155)
SIN_COEFS = (6.2830558, -41.33121429, 81.36681496, -74.47800249, 32.78139661)
SIN_LEAD = SIN_COEFS[4]
SIN_TERMS = tuple(c / SIN_LEAD for c in SIN_COEFS[3::-1])

VMEM_SPEC = pl.BlockSpec(memory_space=pltpu.VMEM)
SMEM_SPEC = pl.BlockSpec(memory_space=pltpu.SMEM)
ANY_SPEC = pl.BlockSpec(memory_space=pl.ANY)


def split3(x):
    hi = x.astype(jnp.bfloat16)
    rest = x - hi.astype(jnp.float32)
    mid = rest.astype(jnp.bfloat16)
    low = (rest - mid.astype(jnp.float32)).astype(jnp.bfloat16)
    return hi, mid, low


def block_start(block, cells):
    count = lax.axis_size("cell")
    return lax.rem(lax.axis_index("cell") + block, count) * cells


def valid_column(block, cells, length):
    position = lax.broadcasted_iota(jnp.int32, (cells, 1), 0) + block_start(block, cells)
    return (position < length).astype(jnp.float32)


def turn_weights_kernel(freq_hbm, phase_hbm, w_ref, freq_ref, phase_buf, sems):
    depth, width = freq_ref.shape
    start = pl.multiple_of(lax.axis_index("cell") * width, BLOCK)
    freq_copy = pltpu.make_async_copy(freq_hbm.at[:, pl.ds(start, width)], freq_ref, sems.at[0])
    phase_copy = pltpu.make_async_copy(phase_hbm.at[:, pl.ds(start, width)], phase_buf, sems.at[1])
    freq_copy.start()
    phase_copy.start()
    freq_copy.wait()
    phase_copy.wait()
    turn = 1.0 / (2.0 * math.pi)
    for part, rows in enumerate(split3(freq_ref[...].astype(jnp.float32) * turn)):
        w_ref[part * depth : (part + 1) * depth, :] = rows
    tail = DEPTH - 3 * depth
    hi, mid, low = [p.astype(jnp.float32) for p in split3(phase_buf[...] * turn)]
    row = lax.broadcasted_iota(jnp.int32, (tail, width), 0)
    rows = jnp.where(row == 0, hi, jnp.where(row == 1, mid, jnp.where(row == 2, low, 0.0)))
    w_ref[3 * depth :, :] = rows.astype(jnp.bfloat16)


def cosine_kernel(blocks, length_ref, w_ref, *refs):
    z_refs, (x_ref, out_ref, mean_ref) = refs[:blocks], refs[blocks:]
    cells, depth = z_refs[0].shape
    width = w_ref.shape[1]
    length = length_ref[0]
    for block in range(blocks):
        valid = valid_column(block, cells, length)
        rows = (z_refs[block][...].astype(jnp.float32) * valid).astype(jnp.bfloat16)
        here = pl.ds(block * cells, cells)
        for part in range(3):
            x_ref[here, part * depth : (part + 1) * depth] = rows
        lane = lax.broadcasted_iota(jnp.int32, (cells, DEPTH - 3 * depth), 1)
        x_ref[here, 3 * depth :] = jnp.where(lane < 3, valid, 0.0).astype(jnp.bfloat16)
    total_rows = blocks * cells
    scale = math.sqrt(2.0 / (width * lax.axis_size("cell")))
    per_length = 1.0 / jnp.full((1, 1), length, jnp.float32)
    a, b, c = COS_TERMS
    strip = mean_ref.shape[1]
    for offset in range(0, width, BLOCK):
        t = jnp.dot(
            x_ref[...], w_ref[:, offset : offset + BLOCK], preferred_element_type=jnp.float32
        )
        r = t - jnp.round(t)
        u = r * r
        s = r * (((u + a) * u + b) * u + c)
        squares = jnp.sum((s * s).reshape(total_rows // SUBLANES, SUBLANES, BLOCK), axis=0)
        squares = jnp.sum(squares, axis=0, keepdims=True)
        mean = scale - (2.0 * scale * COS_LEAD * COS_LEAD) * per_length * squares
        for piece in range(0, BLOCK, 128):
            row, column = divmod(offset + piece, strip)
            mean_ref[row : row + 1, column : column + 128] = mean[:, piece : piece + 128]
    mean = mean_ref[...]
    for study in range(out_ref.shape[0]):
        out_ref[study] = mean


def sine_kernel(x_ref, w_ref, *s_refs):
    cells = s_refs[0].shape[0]
    width = w_ref.shape[1]
    a, b, c, d = SIN_TERMS
    for offset in range(0, width, BLOCK):
        t = jnp.dot(
            x_ref[...], w_ref[:, offset : offset + BLOCK], preferred_element_type=jnp.float32
        )
        r = t - jnp.round(t)
        u = r * r
        s = (r * ((((u + a) * u + b) * u + c) * u + d)).astype(jnp.bfloat16)
        for block, s_ref in enumerate(s_refs):
            s_ref[:, offset : offset + BLOCK] = s[block * cells : (block + 1) * cells]


def coupling_kernel(blocks, length_ref, weight_ref, *refs):
    z_refs, donor_refs, out_ref = refs[:blocks], refs[blocks : 2 * blocks], refs[2 * blocks]
    cells, depth = out_ref.shape
    window = blocks * cells
    length = length_ref[0]
    weight = jnp.full((1, 1), weight_ref[0], jnp.float32)
    inverse_n = 1.0 / jnp.full((1, 1), length, jnp.float32)
    label = lax.broadcasted_iota(jnp.int32, (DONOR_LABELS, cells), 0)
    lane = lax.broadcasted_iota(jnp.int32, (1, cells), 1)
    members, valids = [], []
    counts = jnp.zeros((DONOR_LABELS, 1), jnp.float32)
    for block in range(blocks):
        member = (donor_refs[block][...] == label).astype(jnp.float32)
        valid = (lane + block_start(block, cells) < length).astype(jnp.float32)
        counts = counts + jnp.sum(member * valid, axis=1, keepdims=True)
        members.append(member)
        valids.append(valid)
    inverse = 1.0 / jnp.maximum(counts, 1.0)
    present = jnp.sum((counts > 0.5).astype(jnp.float32), axis=0, keepdims=True)
    row = lax.broadcasted_iota(jnp.int32, (DONOR_LABELS, cells), 0)
    own_inverse = jnp.sum(members[0] * inverse, axis=0, keepdims=True)
    left_same = jnp.concatenate(split3(members[0] * (weight * inverse * inverse)), axis=0)
    bh, bm, bl = [p.astype(jnp.float32) for p in split3(-(weight * inverse_n) * own_inverse)]
    ones = (row < 6).astype(jnp.float32)
    left_rest = jnp.where(row == 0, bh, jnp.where(row == 1, bm, jnp.where(row == 2, bl, ones)))
    left = jnp.concatenate([left_same, left_rest.astype(jnp.bfloat16)], axis=0)
    own = z_refs[0][...]
    own_wide = own.astype(jnp.float32)
    own_sq = jnp.sum(own_wide * own_wide, axis=1, keepdims=True)
    pick = jnp.ones((SUBLANES, depth), jnp.bfloat16)
    total = jnp.zeros((cells, 2 * depth), jnp.float32)
    minor = (((1,), (1,)), ((), ()))
    major = (((0,), (0,)), ((), ()))
    for block in range(blocks):
        member, valid = members[block], valids[block]
        right_inverse = jnp.sum(member * inverse, axis=0, keepdims=True)
        rest = weight * valid * inverse_n * (present * inverse_n - right_inverse)
        ch, cm, cl = [p.astype(jnp.float32) for p in split3(rest)]
        right_rest = jnp.where(
            row < 3,
            valid,
            jnp.where(row == 3, ch, jnp.where(row == 4, cm, jnp.where(row == 5, cl, 0.0))),
        ).astype(jnp.bfloat16)
        same = (member * valid).astype(jnp.bfloat16)
        right = jnp.concatenate([same, same, same, right_rest], axis=0)
        pair_weight = lax.dot_general(left, right, major, preferred_element_type=jnp.float32)
        z = z_refs[block][...]
        wide = z.astype(jnp.float32)
        square = wide * wide
        square_hi = square.astype(jnp.bfloat16)
        square_low = (square - square_hi.astype(jnp.float32)).astype(jnp.bfloat16)
        right_sq = lax.dot_general(
            pick, square_hi, minor, preferred_element_type=jnp.float32
        ) + lax.dot_general(pick, square_low, minor, preferred_element_type=jnp.float32)
        inner = lax.dot_general(own, z, minor, preferred_element_type=jnp.float32)
        squared = own_sq + right_sq[0:1] - 2.0 * inner
        coupling = pair_weight * jnp.exp(squared * (-0.5 / depth))
        hi = coupling.astype(jnp.bfloat16)
        low = (coupling - hi.astype(jnp.float32)).astype(jnp.bfloat16)
        right_rows = jnp.concatenate([z, jnp.ones((cells, depth), jnp.bfloat16)], axis=1)
        total = total + jnp.dot(hi, right_rows, preferred_element_type=jnp.float32)
        total = total + jnp.dot(low, right_rows, preferred_element_type=jnp.float32)
    row_sums = total[:, depth : depth + 1]
    own_valid = valid_column(0, cells, length)
    scale = -(2.0 * window / depth)
    out_ref[...] = scale * own_valid * (own_wide * row_sums - total[:, :depth])


def feature_part(block, length_ref, s_ref, rf_ref, window, width):
    cells = s_ref.shape[0]
    depth = rf_ref.shape[0] // 2
    both = lax.dot_general(
        s_ref[...], rf_ref[...], (((1,), (1,)), ((), ())), preferred_element_type=jnp.float32
    )
    scale = SIN_LEAD * window * math.sqrt(2.0 / (width * lax.axis_size("cell")))
    length = length_ref[0]
    factor = -scale / jnp.full((1, 1), length, jnp.float32)
    return factor * valid_column(block, cells, length) * (both[:, :depth] + both[:, depth:])


def residual_kernel(block, window, length_ref, gathered_ref, mean_ref, freq_ref, s_ref, out_ref, rf_ref):
    studies, _, strip = gathered_ref.shape
    depth, width = freq_ref.shape
    center = gathered_ref[0]
    for study in range(1, studies):
        center = center + gathered_ref[study]
    residual = (2.0 * FEATURE_PENALTY) * (mean_ref[0] - center * (1.0 / studies))
    for row in range(SUBLANES):
        here = slice(row * strip, (row + 1) * strip)
        rows = freq_ref[:, here].astype(jnp.float32) * residual[row : row + 1]
        hi = rows.astype(jnp.bfloat16)
        rf_ref[:depth, here] = hi
        rf_ref[depth:, here] = (rows - hi.astype(jnp.float32)).astype(jnp.bfloat16)
    out_ref[...] = feature_part(block, length_ref, s_ref, rf_ref, window, width)


def own_kernel(window, length_ref, s_ref, rf_ref, base_ref, out_ref):
    width = rf_ref.shape[1]
    out_ref[...] = base_ref[...] + feature_part(0, length_ref, s_ref, rf_ref, window, width)


def call(kernel, out_shape, in_specs, name, flops, transcendentals=0, size=0, scratch=(), vmem=32):
    several = isinstance(out_shape, (list, tuple))
    return pl.pallas_call(
        kernel,
        out_shape=out_shape,
        in_specs=in_specs,
        out_specs=[VMEM_SPEC] * len(out_shape) if several else VMEM_SPEC,
        scratch_shapes=list(scratch),
        compiler_params=pltpu.CompilerParams(vmem_limit_bytes=vmem * MIB),
        cost_estimate=pl.CostEstimate(
            flops=int(flops), bytes_accessed=int(size), transcendentals=int(transcendentals)
        ),
        name=name,
    )


def rotated(x, shift):
    count = lax.axis_size("cell")
    return lax.ppermute(x, "cell", [((i + shift) % count, i) for i in range(count)])


def on_device(latents, donor_ids, study_valid_length, study_penalty_weight, frequencies, phases):
    own = latents[0]
    cells, depth = own.shape
    blocks = lax.axis_size("cell")
    studies = lax.axis_size("study")
    features = frequencies.shape[1]
    width = features // blocks
    window = blocks * cells
    strip = width // SUBLANES
    f32, bf16 = jnp.float32, jnp.bfloat16
    shape = jax.ShapeDtypeStruct
    pairs = window * width

    rows = [own] + [rotated(own, k) for k in range(1, blocks)]
    donors = [donor_ids] + [rotated(donor_ids, k) for k in range(1, blocks)]

    turn_weights, freq_part = call(
        turn_weights_kernel,
        [shape((DEPTH, width), bf16), shape((depth, width), bf16)],
        [ANY_SPEC, ANY_SPEC],
        "turn_weights",
        flops=20 * depth * width,
        size=4 * depth * width,
        scratch=[pltpu.VMEM((1, width), f32), pltpu.SemaphoreType.DMA((2,))],
    )(frequencies, phases.reshape(1, features))

    x, copies = call(
        functools.partial(cosine_kernel, blocks),
        [shape((window, DEPTH), bf16), shape((studies, SUBLANES, strip), f32)],
        [SMEM_SPEC] + [VMEM_SPEC] * (1 + blocks),
        "cosine_sums",
        flops=2 * DEPTH * pairs + 12 * pairs,
        size=2 * DEPTH * width,
        scratch=[pltpu.VMEM((SUBLANES, strip), f32)],
    )(study_valid_length, turn_weights, *rows)

    gathered = lax.all_to_all(copies, "study", 0, 0, tiled=True)

    sines = call(
        sine_kernel,
        [shape((cells, width), bf16)] * blocks,
        [VMEM_SPEC] * 2,
        "sines",
        flops=2 * DEPTH * pairs + 12 * pairs,
        size=2 * pairs,
    )(x, turn_weights)
    base = call(
        functools.partial(coupling_kernel, blocks),
        shape((cells, depth), f32),
        [SMEM_SPEC] * 2 + [VMEM_SPEC] * (2 * blocks),
        "coupling",
        flops=2 * cells * window * (3 * depth),
        transcendentals=cells * window,
        size=4 * cells * depth,
    )(study_valid_length, study_penalty_weight, *rows, *donors)

    out = None
    residual_freq = None
    for block in range(1, blocks):
        if residual_freq is None:
            part, residual_freq = call(
                functools.partial(residual_kernel, block, window),
                [shape((cells, depth), f32), shape((2 * depth, width), bf16)],
                [SMEM_SPEC] + [VMEM_SPEC] * 4,
                "residual_part",
                flops=2 * cells * width * depth,
                size=2 * cells * width,
            )(study_valid_length, gathered, copies[:1], freq_part, sines[block])
        else:
            part = call(
                functools.partial(other_kernel, block, window),
                shape((cells, depth), f32),
                [SMEM_SPEC] + [VMEM_SPEC] * 2,
                "other_part",
                flops=2 * cells * width * depth,
                size=2 * cells * width,
            )(study_valid_length, sines[block], residual_freq)
        sent = rotated(part, blocks - block)
        out = sent if out is None else out + sent
    own_part = call(
        functools.partial(own_kernel, window),
        shape((cells, depth), f32),
        [SMEM_SPEC] + [VMEM_SPEC] * 3,
        "own_part",
        flops=2 * cells * width * depth,
        size=2 * cells * width,
    )(study_valid_length, sines[0], residual_freq, base)
    return (own_part + out)[None]


def other_kernel(block, window, length_ref, s_ref, rf_ref, out_ref):
    width = rf_ref.shape[1]
    out_ref[...] = feature_part(block, length_ref, s_ref, rf_ref, window, width)


def solution(mesh):
    in_specs = (P("study", "cell", None), P("study", "cell"), P("study"), P("study"), P(), P())
    out_specs = P("study", "cell", None)
    return jax.shard_map(
        on_device, mesh=mesh, in_specs=in_specs, out_specs=out_specs, check_vma=False
    )
```

profile of v0, /device:TPU:0, one launch (start us, length us, event | category | flops | bytes accessed | tf_op | source)
XLA Modules:
  0.0 42.4 jit_solution(13633270584348595217)
XLA Ops:
  0.0 1.0 %copy.7 = bf16[1,512,64]{2,1,0:T(8,128)(2,1)S(1)} copy(bf16[1,512,64]{1,2,0:T(8,128)(2,1)} %param.6) | data formatting | bytes 131072 | tf_op args[0]
  1.0 0.5 %collective-permute-start = (bf16[512,64]{1,0:T(8,128)(2,1)S(1)}, bf16[512,64]{1,0:T(8,128)(2,1)S(1)}, u32[]{:S(2)}, u32[]{:S(2)}) collective-permute-start(bf16[512,64]{1,0:T(8,128)(2,1)S(1)} %bitcast.4), channel_id=1, source_target_pairs={{1,0},{0,1},{3,2},{2,3},{5,4},{4,5},{7,6},{6,7},{9,8},{8,9},{11,10... | collective-permute-start | bytes 196616 | tf_op jit(solution)/shard_map/ppermute | solution.py:236
  2.1 0.0 copy-start.4
  2.1 1.2 %copy-done.4 = bf16[64,8192]{1,0:T(8,128)(2,1)S(1)} copy-done((bf16[64,8192]{1,0:T(8,128)(2,1)S(1)}, bf16[64,8192]{1,0:T(8,128)(2,1)}, u32[]{:S(2)}) %copy-start.4) | copy-done | bytes 1048600
  3.4 0.8 %copy-done.5 = f32[8192]{0:T(1024)S(1)} copy-done((f32[8192]{0:T(1024)S(1)}, f32[8192]{0:T(1024)}, u32[]{:S(2)}) %copy-start.5) | copy-done | bytes 32792
  4.1 0.5 %turn_weights.1 = (bf16[256,4096]{1,0:T(8,128)(2,1)S(1)}, bf16[64,4096]{1,0:T(8,128)(2,1)S(1)}) custom-call(bf16[64,8192]{1,0:T(8,128)(2,1)S(1)} %copy-done.4, f32[1,8192]{1,0:T(1,128)S(1)} %bitcast.7), custom_call_target="tpu_custom_call" | custom-call | flops 5242880 | bytes 1048576 | tf_op jit(solution)/shard_map/turn_weights/pallas_call | solution.py:255
  4.6 0.0 collective-permute-done.refs_1_
  4.6 7.3 %cosine_sums.1 = (bf16[1024,256]{1,0:T(8,128)(2,1)S(1)}, f32[16,8,512]{2,1,0:T(8,128)}) custom-call(s32[1]{0:T(128)S(6)} %copy.9.length_ref, bf16[256,4096]{1,0:T(8,128)(2,1)S(1)} %get-tuple-element.13.w_ref, bf16[512,64]{1,0:T(8,128)(2,1)S(1)} %bitcast.5, bf16[512,64]{1,0:T(8,128)(2,1)S(1)} %collective-permute-done.refs_1_), custom_call_target="tpu_custom_call" | custom-call | flops 2197815296 | bytes 2097152 | tf_op jit(solution)/shard_map/cosine_sums/pallas_call | solution.py:265
  11.9 0.8 %copy-done.7 = bf16[1024,256]{1,0:T(8,128)(2,1)} copy-done((bf16[1024,256]{1,0:T(8,128)(2,1)}, bf16[1024,256]{1,0:T(8,128)(2,1)S(1)}, u32[]{:S(2)}) %copy-start.7) | copy-done | bytes 524312
  12.7 7.9 %all-to-all-start = ((f32[16,8,512]{2,1,0:T(8,128)}), f32[16,8,512]{2,1,0:T(8,128)S(1)}, u32[]{:S(2)}, u32[]{:S(2)}) async-start(f32[16,8,512]{2,1,0:T(8,128)} %get-tuple-element.16), calls=%async_computation | async-start | bytes 524288 | tf_op jit(solution)/shard_map/all_to_all | solution.py:275
  20.6 0.7 %slice.3.mean_ref = f32[1,8,512]{2,1,0:T(8,128)S(1)} slice(f32[16,8,512]{2,1,0:T(8,128)} %get-tuple-element.16), slice={[0:1], [0:8], [0:512]} | slice | bytes 32768 | tf_op jit(solution)/shard_map/slice | solution.py:306
  21.3 1.0 %copy-done.8 = bf16[1024,256]{1,0:T(8,128)(2,1)S(1)} copy-done((bf16[1024,256]{1,0:T(8,128)(2,1)S(1)}, bf16[1024,256]{1,0:T(8,128)(2,1)}, u32[]{:S(2)}) %copy-start.8) | copy-done | bytes 524312
  22.3 6.5 %sines.1 = (bf16[512,4096]{1,0:T(8,128)(2,1)S(1)}, bf16[512,4096]{1,0:T(8,128)(2,1)S(1)}) custom-call(bf16[1024,256]{1,0:T(8,128)(2,1)S(1)} %copy-done.8, bf16[256,4096]{1,0:T(8,128)(2,1)S(1)} %get-tuple-element.13.w_ref), custom_call_target="tpu_custom_call" | custom-call | flops 2197815296 | bytes 8388608 | tf_op jit(solution)/shard_map/sines/pallas_call | solution.py:277
  28.9 2.0 %copy-done = bf16[512,4096]{1,0:T(8,128)(2,1)} copy-done((bf16[512,4096]{1,0:T(8,128)(2,1)}, bf16[512,4096]{1,0:T(8,128)(2,1)S(1)}, u32[]{:S(2)}) %copy-start) | copy-done | bytes 4194328
  30.8 2.0 %copy-done.2 = bf16[512,4096]{1,0:T(8,128)(2,1)} copy-done((bf16[512,4096]{1,0:T(8,128)(2,1)}, bf16[512,4096]{1,0:T(8,128)(2,1)S(1)}, u32[]{:S(2)}) %copy-start.2) | copy-done | bytes 4194328
  32.8 0.0 all-to-all-done.gathered_ref
  32.8 2.2 %copy-done.1 = bf16[512,4096]{1,0:T(8,128)(2,1)S(1)} copy-done((bf16[512,4096]{1,0:T(8,128)(2,1)S(1)}, bf16[512,4096]{1,0:T(8,128)(2,1)}, u32[]{:S(2)}) %copy-start.1) | copy-done | bytes 4194328
  35.0 1.3 %residual_part.1 = (f32[512,64]{1,0:T(8,128)S(1)}, bf16[128,4096]{1,0:T(8,128)(2,1)S(1)}) custom-call(s32[1]{0:T(128)S(6)} %copy.9.length_ref, f32[16,8,512]{2,1,0:T(8,128)S(1)} %all-to-all-done.gathered_ref, f32[1,8,512]{2,1,0:T(8,128)S(1)} %slice.3.mean_ref, bf16[64,4096]{1,0:T(8,128)(2,1)S(1)} %get-tuple-element.17.freq_ref, bf16[512,4096]{1,0:T(8,128)(2,1)S(1)} %copy-done.1), custom_call_target="tpu_custom_call" | custom-call | flops 268435456 | bytes 4194304 | tf_op jit(solution)/shard_map/residual_part/pallas_call | solution.py:299
  36.3 0.3 collective-permute-start.2
  36.6 0.3 collective-permute-start.1
  37.6 0.4 collective-permute-done.1.refs_3_
  37.9 2.3 %coupling.1.base_ref = f32[512,64]{1,0:T(8,128)S(1)} custom-call(s32[1]{0:T(128)S(6)} %copy.9.length_ref, f32[1]{0:T(128)S(6)} %copy.10.weight_ref, bf16[512,64]{1,0:T(8,128)(2,1)S(1)} %bitcast.6, bf16[512,64]{1,0:T(8,128)(2,1)S(1)} %collective-permute-done.refs_1_, s32[1,512]{1,0:T(1,128)S(1)} %copy-done.6, s32[1,512]{1,0:T(1,128)S(1)} %collective-permute-done.1.refs_3_), custom_call_target="tpu_custom_call" | custom-call | flops 201326592 | bytes 131072 | tf_op jit(solution)/shard_map/coupling/pallas_call | solution.py:285
  40.3 1.3 %own_part.1 = f32[512,64]{1,0:T(8,128)S(1)} custom-call(s32[1]{0:T(128)S(6)} %copy.9.length_ref, bf16[512,4096]{1,0:T(8,128)(2,1)S(1)} %copy-done.3, bf16[128,4096]{1,0:T(8,128)(2,1)S(1)} %get-tuple-element.19.rf_ref, f32[512,64]{1,0:T(8,128)S(1)} %coupling.1.base_ref), custom_call_target="tpu_custom_call" | custom-call | flops 268435456 | bytes 4194304 | tf_op jit(solution)/shard_map/own_part/pallas_call | solution.py:318
  41.6 0.8 %copy.8 = f32[1,512,64]{1,2,0:T(8,128)} copy(f32[1,512,64]{2,1,0:T(8,128)S(1)} %add_bitcast_fusion) | data formatting | bytes 262144 | tf_op jit(solution)/shard_map/broadcast_in_dim | solution.py:326
  (12 shorter events, 0.0 us)
Async XLA Ops:
  1.0 3.7 %collective-permute-start = (bf16[512,64]{1,0:T(8,128)(2,1)S(1)}, bf16[512,64]{1,0:T(8,128)(2,1)S(1)}, u32[]{:S(2)}, u32[]{:S(2)}) collective-permute-start(bf16[512,64]{1,0:T(8,128)(2,1)S(1)} %bitcast.4), channel_id=1, source_target_pairs={{1,0},{0,1},{3,2},{2,3},{5,4},{4,5},{7,6},{6,7},{9,8},{8,9},{11,10... | collective-permute-start | bytes 196616 | tf_op jit(solution)/shard_map/ppermute | solution.py:236
  2.1 1.2 %copy-start.4 = (bf16[64,8192]{1,0:T(8,128)(2,1)S(1)}, bf16[64,8192]{1,0:T(8,128)(2,1)}, u32[]{:S(2)}) copy-start(bf16[64,8192]{1,0:T(8,128)(2,1)} %freq_hbm.1) | copy-start | bytes 3145732
  3.4 0.8 %copy-start.5 = (f32[8192]{0:T(1024)S(1)}, f32[8192]{0:T(1024)}, u32[]{:S(2)}) copy-start(f32[8192]{0:T(1024)} %param.11) | copy-start | bytes 98308
  11.9 0.8 %copy-start.7 = (bf16[1024,256]{1,0:T(8,128)(2,1)}, bf16[1024,256]{1,0:T(8,128)(2,1)S(1)}, u32[]{:S(2)}) copy-start(bf16[1024,256]{1,0:T(8,128)(2,1)S(1)} %get-tuple-element.14.x_ref) | copy-start | bytes 1572868
  12.7 20.1 %all-to-all-start = ((f32[16,8,512]{2,1,0:T(8,128)}), f32[16,8,512]{2,1,0:T(8,128)S(1)}, u32[]{:S(2)}, u32[]{:S(2)}) async-start(f32[16,8,512]{2,1,0:T(8,128)} %get-tuple-element.16), calls=%async_computation | async-start | bytes 524288 | tf_op jit(solution)/shard_map/all_to_all | solution.py:275
  21.3 1.0 %copy-start.8 = (bf16[1024,256]{1,0:T(8,128)(2,1)S(1)}, bf16[1024,256]{1,0:T(8,128)(2,1)}, u32[]{:S(2)}) copy-start(bf16[1024,256]{1,0:T(8,128)(2,1)} %copy-done.7) | copy-start | bytes 1572868
  28.8 2.0 %copy-start = (bf16[512,4096]{1,0:T(8,128)(2,1)}, bf16[512,4096]{1,0:T(8,128)(2,1)S(1)}, u32[]{:S(2)}) copy-start(bf16[512,4096]{1,0:T(8,128)(2,1)S(1)} %get-tuple-element.18.s_ref) | copy-start | bytes 12582916
  30.8 2.0 %copy-start.2 = (bf16[512,4096]{1,0:T(8,128)(2,1)}, bf16[512,4096]{1,0:T(8,128)(2,1)S(1)}, u32[]{:S(2)}) copy-start(bf16[512,4096]{1,0:T(8,128)(2,1)S(1)} %get-tuple-element.15.s_ref) | copy-start | bytes 12582916
  32.8 3.8 %copy-start.6 = (s32[1,512]{1,0:T(1,128)S(1)}, s32[1,512]{1,0:T(1,128)}, u32[]{:S(2)}) copy-start(s32[1,512]{1,0:T(1,128)} %refs_2_.1) | copy-start | bytes 6148
  32.8 2.2 %copy-start.1 = (bf16[512,4096]{1,0:T(8,128)(2,1)S(1)}, bf16[512,4096]{1,0:T(8,128)(2,1)}, u32[]{:S(2)}) copy-start(bf16[512,4096]{1,0:T(8,128)(2,1)} %copy-done) | copy-start | bytes 12582916
  35.0 5.3 %copy-start.3 = (bf16[512,4096]{1,0:T(8,128)(2,1)S(1)}, bf16[512,4096]{1,0:T(8,128)(2,1)}, u32[]{:S(2)}) copy-start(bf16[512,4096]{1,0:T(8,128)(2,1)} %copy-done.2) | copy-start | bytes 12582916
  36.3 5.3 %collective-permute-start.2 = (f32[512,64]{1,0:T(8,128)S(1)}, f32[512,64]{1,0:T(8,128)S(1)}, u32[]{:S(2)}, u32[]{:S(2)}) collective-permute-start(f32[512,64]{1,0:T(8,128)S(1)} %get-tuple-element.20), channel_id=1, source_target_pairs={{1,0},{0,1},{3,2},{2,3},{5,4},{4,5},{7,6},{6,7},{9,8},{8,9},{11,10... | collective-permute-start | bytes 393224 | tf_op jit(solution)/shard_map/ppermute | solution.py:236
  36.6 1.3 %collective-permute-start.1 = (s32[1,512]{1,0:T(1,128)S(1)}, s32[1,512]{1,0:T(1,128)S(1)}, u32[]{:S(2)}, u32[]{:S(2)}) collective-permute-start(s32[1,512]{1,0:T(1,128)S(1)} %copy-done.6), channel_id=1, source_target_pairs={{1,0},{0,1},{3,2},{2,3},{5,4},{4,5},{7,6},{6,7},{9,8},{8,9},{11,10... | collective-permute-start | bytes 6152 | tf_op jit(solution)/shard_map/ppermute | solution.py:236
where the time goes:
time: 42.9 us; the launch traced here: 42.4 us
  Pallas kernels  19.2 us (45%)
  local copies, waits for them, and re-layouts  12.4 us (29%)
  starting transfers between devices  8.97 us (21%)
  between operations  1.4 us (3%)
    unnamed x19, local copies, waits for them, and re-layouts  10.9 us
    all_to_all x1, starting transfers between devices, on_device(): gathered = lax.all_to_all(copies, 'study', 0, 0, tiled=True)  7.88 us
    pallas_call x1, Pallas kernels, on_device(): call(functools.partial(cosine_kernel, blocks), [shape((window, DEPTH), bf...  7.25 us
    pallas_call x1, Pallas kernels, on_device(): call(sine_kernel, [shape((cells, width), bf16)] * blocks, [VMEM_SPEC] * 2...  6.52 us
    pallas_call x1, Pallas kernels, on_device(): call(functools.partial(coupling_kernel, blocks), shape((cells, depth), f3...  2.32 us
    pallas_call x1, Pallas kernels, on_device(): call(functools.partial(residual_kernel, block, window), [shape((cells, de...  1.34 us
    pallas_call x1, Pallas kernels, on_device(): call(functools.partial(own_kernel, window), shape((cells, depth), f32), [...  1.32 us
    ppermute x3, starting transfers between devices, rotated(): lax.ppermute(x, 'cell', [((i + shift) % count, i) for i in range(count)])  1.09 us
  transfers between devices with their start and end apart: 4, of which 1 were waited for; matrix products, arithmetic and copies ran while one was open for 2% of the time, Pallas kernels for 25%

commit v1 on v0

v1 whole, which is shorter than its diff:
```python
import functools
import math

import jax
import jax.numpy as jnp
from jax import lax
from jax.experimental import pallas as pl
from jax.experimental.pallas import tpu as pltpu
from jax.sharding import PartitionSpec as P

DONOR_LABELS = 16
FEATURE_PENALTY = 16.0
BLOCK = 256
PAIR = 128
SUBLANES = 8
MIB = 1 << 20

COS_LEAD = -0.552051508388134
COS_TERMS = (-4.602194203577409, 9.359560663732573, -5.6907268683441155)
SIN_LEAD = 2.0 * COS_LEAD * abs(COS_LEAD)

VMEM_SPEC = pl.BlockSpec(memory_space=pltpu.VMEM)
HBM_SPEC = pl.BlockSpec(memory_space=pltpu.HBM)


def split3(x):
    hi = x.astype(jnp.bfloat16)
    rest = x - hi.astype(jnp.float32)
    mid = rest.astype(jnp.bfloat16)
    low = (rest - mid.astype(jnp.float32)).astype(jnp.bfloat16)
    return hi, mid, low


def block_start(block, cells):
    count = lax.axis_size("cell")
    return lax.rem(lax.axis_index("cell") + block, count) * cells


def valid_row(block, cells, length):
    position = lax.broadcasted_iota(jnp.int32, (1, cells), 1) + block_start(block, cells)
    return (position.astype(jnp.float32) < length).astype(jnp.float32)


def feature_scale(width):
    return math.sqrt(2.0 / (width * lax.axis_size("cell")))


def store_rows(x_ref, z, valid):
    depth, cells = z.shape
    z = z.astype(jnp.float32) * valid
    tail = 2 * PAIR - 3 * depth
    ones = jnp.where(lax.broadcasted_iota(jnp.int32, (tail, cells), 0) < 3, valid, 0.0)
    x_ref[:, :PAIR] = jnp.concatenate([z, z], axis=0).T.astype(jnp.bfloat16)
    x_ref[:, PAIR:] = jnp.concatenate([z, ones], axis=0).T.astype(jnp.bfloat16)


def setup_kernel(const_ref, freq_hbm, phase_hbm, z_hbm, w_ref, freq_ref, z_ref, x_ref, phase_buf, sems):
    depth, width = freq_ref.shape
    start = pl.multiple_of(lax.axis_index("cell") * width, BLOCK)
    copies = [
        pltpu.make_async_copy(source, target, sems.at[i])
        for i, (source, target) in enumerate(
            [
                (z_hbm, z_ref),
                (phase_hbm.at[:, pl.ds(start, width)], phase_buf),
                (freq_hbm.at[:, pl.ds(start, width)], freq_ref),
            ]
        )
    ]
    for copy in copies:
        copy.start()
    copies[0].wait()
    length = const_ref[0:1, 0:1]
    store_rows(x_ref, z_ref[...], valid_row(0, z_ref.shape[1], length))
    for copy in copies[1:]:
        copy.wait()
    turn = 1.0 / (2.0 * math.pi)
    for part, rows in enumerate(split3(freq_ref[...].astype(jnp.float32) * turn)):
        w_ref[part * depth : (part + 1) * depth, :] = rows
    tail = 2 * PAIR - 3 * depth
    hi, mid, low = [p.astype(jnp.float32) for p in split3(phase_buf[...] * turn)]
    row = lax.broadcasted_iota(jnp.int32, (tail, width), 0)
    rows = jnp.where(row == 0, hi, jnp.where(row == 1, mid, jnp.where(row == 2, low, 0.0)))
    w_ref[3 * depth :, :] = rows.astype(jnp.bfloat16)


def cosine_kernel(blocks, const_ref, w_ref, x_own_ref, *refs):
    z_refs = refs[: blocks - 1]
    s_refs = refs[blocks - 1 : 2 * blocks - 1]
    mean_ref = refs[2 * blocks - 1]
    x_refs = [x_own_ref, *refs[2 * blocks :]]
    cells, width = s_refs[0].shape
    length = const_ref[0:1, 0:1]
    for block in range(1, blocks):
        store_rows(x_refs[block], z_refs[block - 1][...], valid_row(block, cells, length))
    scale = feature_scale(width)
    per_length = 1.0 / length
    a, b, c = COS_TERMS
    strip = mean_ref.shape[1]
    for offset in range(0, width, BLOCK):
        here = slice(offset, offset + BLOCK)
        squares = jnp.zeros((SUBLANES, BLOCK), jnp.float32)
        for x_ref, s_ref in zip(x_refs, s_refs):
            t = jnp.dot(x_ref[...], w_ref[:, here], preferred_element_type=jnp.float32)
            r = t - jnp.round(t)
            u = r * r
            s = r * (((u + a) * u + b) * u + c)
            s_ref[:, here] = s
            squares += jnp.sum((s * s).reshape(cells // SUBLANES, SUBLANES, BLOCK), axis=0)
        squares = jnp.sum(squares, axis=0, keepdims=True)
        mean = scale - (2.0 * scale * COS_LEAD * COS_LEAD) * per_length * squares
        for piece in range(0, BLOCK, 128):
            row, column = divmod(offset + piece, strip)
            mean_ref[row : row + 1, column : column + 128] = mean[:, piece : piece + 128]


def sine_kernel(blocks, *refs):
    top = (1.0 + 2e-6) / (COS_LEAD * COS_LEAD)
    cells, width = refs[0].shape
    for s_ref, out_ref in zip(refs[:blocks], refs[blocks:]):
        for offset in range(0, width, BLOCK):
            here = slice(offset, offset + BLOCK)
            s = s_ref[:, here]
            rest = top - s * s
            out_ref[:, here] = (s * (rest * lax.rsqrt(rest))).astype(jnp.bfloat16)


def coupling_kernel(blocks, const_ref, *refs):
    z_refs, donor_refs, out_ref = refs[:blocks], refs[blocks : 2 * blocks], refs[2 * blocks]
    depth, cells = out_ref.shape
    window = blocks * cells
    length = const_ref[0:1, 0:1]
    weight = const_ref[1:2, 0:1]
    inverse_n = 1.0 / length
    label = lax.broadcasted_iota(jnp.int32, (DONOR_LABELS, cells), 0)
    members, valids = [], []
    counts = jnp.zeros((DONOR_LABELS, 1), jnp.float32)
    for block in range(blocks):
        member = (donor_refs[block][...] == label).astype(jnp.float32)
        valid = valid_row(block, cells, length)
        counts = counts + jnp.sum(member * valid, axis=1, keepdims=True)
        members.append(member)
        valids.append(valid)
    inverse = 1.0 / jnp.maximum(counts, 1.0)
    present = jnp.sum((counts > 0.5).astype(jnp.float32), axis=0, keepdims=True)
    row = lax.broadcasted_iota(jnp.int32, (DONOR_LABELS, cells), 0)
    own_inverse = jnp.sum(members[0] * inverse, axis=0, keepdims=True)
    left_same = jnp.concatenate(split3(members[0] * (weight * inverse * inverse)), axis=0)
    bh, bm, bl = [p.astype(jnp.float32) for p in split3(-(weight * inverse_n) * own_inverse)]
    ones = (row < 6).astype(jnp.float32)
    left_rest = jnp.where(row == 0, bh, jnp.where(row == 1, bm, jnp.where(row == 2, bl, ones)))
    left = jnp.concatenate([left_same, left_rest.astype(jnp.bfloat16)], axis=0)
    own = z_refs[0][...]
    own_wide = own.astype(jnp.float32)
    own_sq = jnp.sum(own_wide * own_wide, axis=0, keepdims=True)
    total = jnp.zeros((cells, PAIR), jnp.float32)
    minor = (((1,), (1,)), ((), ()))
    major = (((0,), (0,)), ((), ()))
    own_column = jnp.broadcast_to(own_sq, (PAIR, cells)).T[:, 0:1]
    for block in range(blocks):
        member, valid = members[block], valids[block]
        right_inverse = jnp.sum(member * inverse, axis=0, keepdims=True)
        rest = weight * valid * inverse_n * (present * inverse_n - right_inverse)
        ch, cm, cl = [p.astype(jnp.float32) for p in split3(rest)]
        right_rest = jnp.where(
            row < 3,
            valid,
            jnp.where(row == 3, ch, jnp.where(row == 4, cm, jnp.where(row == 5, cl, 0.0))),
        ).astype(jnp.bfloat16)
        same = (member * valid).astype(jnp.bfloat16)
        right = jnp.concatenate([same, same, same, right_rest], axis=0)
        pair_weight = lax.dot_general(left, right, major, preferred_element_type=jnp.float32)
        z = z_refs[block][...]
        wide = z.astype(jnp.float32)
        right_sq = jnp.sum(wide * wide, axis=0, keepdims=True)
        inner = lax.dot_general(own, z, major, preferred_element_type=jnp.float32)
        squared = own_column + right_sq - 2.0 * inner
        coupling = pair_weight * jnp.exp(squared * (-0.5 / depth))
        hi = coupling.astype(jnp.bfloat16)
        low = (coupling - hi.astype(jnp.float32)).astype(jnp.bfloat16)
        right_rows = jnp.concatenate([z, jnp.ones((PAIR - depth, cells), jnp.bfloat16)], axis=0)
        for part in (hi, low):
            total = total + lax.dot_general(
                part, right_rows, minor, preferred_element_type=jnp.float32
            )
    total = total.T
    scale = -(2.0 * window / depth)
    own_valid = valid_row(0, cells, length)
    out_ref[...] = scale * own_valid * (own_wide * total[depth : depth + 1] - total[:depth])


def feature_part(block, const_ref, s_ref, rf_ref, window):
    cells, width = s_ref.shape
    depth = rf_ref.shape[0] // 2
    both = lax.dot_general(
        s_ref[...], rf_ref[...], (((1,), (1,)), ((), ())), preferred_element_type=jnp.float32
    ).T
    length = const_ref[0:1, 0:1]
    factor = -(SIN_LEAD * window * feature_scale(width)) / length
    return factor * valid_row(block, cells, length) * (both[:depth] + both[depth:])


def residual_kernel(block, window, const_ref, sum_ref, mean_ref, freq_ref, s_ref, out_ref, rf_ref):
    strip = sum_ref.shape[1]
    depth = freq_ref.shape[0]
    center = sum_ref[...] * (1.0 / lax.axis_size("study"))
    residual = (2.0 * FEATURE_PENALTY) * (mean_ref[...] - center)
    for row in range(SUBLANES):
        here = slice(row * strip, (row + 1) * strip)
        rows = freq_ref[:, here].astype(jnp.float32) * residual[row : row + 1]
        hi = rows.astype(jnp.bfloat16)
        rf_ref[:depth, here] = hi
        rf_ref[depth:, here] = (rows - hi.astype(jnp.float32)).astype(jnp.bfloat16)
    out_ref[...] = feature_part(block, const_ref, s_ref, rf_ref, window)


def other_kernel(block, window, const_ref, s_ref, rf_ref, out_ref):
    out_ref[...] = feature_part(block, const_ref, s_ref, rf_ref, window)


def own_kernel(window, const_ref, s_ref, rf_ref, base_ref, out_ref):
    out_ref[...] = base_ref[...] + feature_part(0, const_ref, s_ref, rf_ref, window)


def call(kernel, out_shape, name, flops, transcendentals=0, size=0, scratch=(), vmem=8, in_specs=None):
    several = isinstance(out_shape, (list, tuple))

    def run(*operands):
        return pl.pallas_call(
            kernel,
            out_shape=out_shape,
            in_specs=in_specs or [VMEM_SPEC] * len(operands),
            out_specs=[VMEM_SPEC] * len(out_shape) if several else VMEM_SPEC,
            scratch_shapes=list(scratch),
            compiler_params=pltpu.CompilerParams(vmem_limit_bytes=vmem * MIB),
            cost_estimate=pl.CostEstimate(
                flops=int(flops), bytes_accessed=int(size), transcendentals=int(transcendentals)
            ),
            name=name,
        )(*operands)

    return run


def rotated(x, shift):
    count = lax.axis_size("cell")
    return lax.ppermute(x, "cell", [((i + shift) % count, i) for i in range(count)])


def digits(count):
    radices = []
    while count > 1:
        radix = next(r for r in (4, 2, *range(3, count + 1)) if count % r == 0)
        radices.append(radix)
        count //= radix
    return radices


def swapped(x, stride, radix):
    count = lax.axis_size("study")

    def partner(i, k):
        digit = i // stride % radix
        other = digit ^ k if radix & (radix - 1) == 0 else (digit + k) % radix
        return i + (other - digit) * stride

    return [
        lax.ppermute(x, "study", [(i, partner(i, k)) for i in range(count)])
        for k in range(1, radix)
    ]


def on_device(latents, donor_ids, study_valid_length, study_penalty_weight, frequencies, phases):
    own = jnp.swapaxes(latents[0], 0, 1)
    depth, cells = own.shape
    blocks = lax.axis_size("cell")
    studies = lax.axis_size("study")
    features = frequencies.shape[1]
    width = features // blocks
    window = blocks * cells
    strip = width // SUBLANES
    f32, bf16 = jnp.float32, jnp.bfloat16
    shape = jax.ShapeDtypeStruct
    pairs = window * width

    others = [rotated(own, k) for k in range(1, blocks)]
    donors = [donor_ids] + [rotated(donor_ids, k) for k in range(1, blocks)]

    consts = jnp.broadcast_to(
        jnp.stack([study_valid_length.astype(f32), study_penalty_weight]), (2, 128)
    )
    in_hbm = [
        pltpu.with_memory_space_constraint(operand, pltpu.HBM)
        for operand in (frequencies, phases.reshape(1, features), own)
    ]
    turn_weights, freq_part, own, x_own = call(
        setup_kernel,
        [
            shape((2 * PAIR, width), bf16),
            shape((depth, width), bf16),
            shape((depth, cells), bf16),
            shape((cells, 2 * PAIR), bf16),
        ],
        "setup",
        flops=20 * depth * width,
        size=4 * depth * width,
        scratch=[pltpu.VMEM((1, width), f32), pltpu.SemaphoreType.DMA((3,))],
        in_specs=[VMEM_SPEC] + [HBM_SPEC] * 3,
    )(consts, *in_hbm)

    *halves, mean = call(
        functools.partial(cosine_kernel, blocks),
        [shape((cells, width), f32)] * blocks + [shape((SUBLANES, strip), f32)],
        "cosine_sums",
        flops=4 * PAIR * pairs + 12 * pairs,
        size=4 * PAIR * width,
        scratch=[pltpu.VMEM((cells, 2 * PAIR), bf16)] * (blocks - 1),
    )(consts, turn_weights, x_own, *others)

    def couplings(z_blocks):
        return call(
            functools.partial(coupling_kernel, blocks),
            shape((depth, cells), f32),
            "coupling",
            flops=2 * cells * window * (3 * depth),
            transcendentals=cells * window,
            size=4 * cells * depth,
        )(consts, *z_blocks, *donors)

    center, base, stride = mean, None, 1
    for radix in digits(studies):
        parts = swapped(center, stride, radix)
        stride *= radix
        if base is None:
            base = couplings([own, *others])
            center = sum(parts, center)
            center, base, *halves = lax.optimization_barrier((center, base, *halves))
        else:
            center = sum(parts, center)
    if base is None:
        base = couplings([own, *others])

    sines = call(
        functools.partial(sine_kernel, blocks),
        [shape((cells, width), bf16)] * blocks,
        "sines",
        flops=12 * pairs,
        transcendentals=pairs,
        size=6 * pairs,
    )(*halves)

    out, residual_freq = None, None
    part_shape = shape((depth, cells), f32)
    cost = dict(flops=2 * cells * width * depth, size=2 * cells * width)
    for block in range(1, blocks):
        if residual_freq is None:
            part, residual_freq = call(
                functools.partial(residual_kernel, block, window),
                [part_shape, shape((2 * depth, width), bf16)],
                "residual_part",
                **cost,
            )(consts, center, mean, freq_part, sines[block])
        else:
            part = call(
                functools.partial(other_kernel, block, window), part_shape, "other_part", **cost
            )(consts, sines[block], residual_freq)
        sent = rotated(part, blocks - block)
        out = sent if out is None else out + sent
    own_part = call(functools.partial(own_kernel, window), part_shape, "own_part", **cost)(
        consts, sines[0], residual_freq, base
    )
    return jnp.swapaxes(own_part + out, 0, 1)[None]


def solution(mesh):
    in_specs = (P("study", "cell", None), P("study", "cell"), P("study"), P("study"), P(), P())
    out_specs = P("study", "cell", None)
    return jax.shard_map(
        on_device, mesh=mesh, in_specs=in_specs, out_specs=out_specs, check_vma=False
    )
```

time: 42.9 us -> 30.1 us (0.70)
  local copies, waits for them, and re-layouts: 12.4 us -> 0.08 us
  Pallas kernels: 19.2 us -> 15.8 us
  waiting for transfers between devices: 0.38 us -> 2.27 us
  other arithmetic: 0.03 us -> 0.76 us
  starting transfers between devices: 8.97 us -> 9.57 us
    unnamed x19 -> x2, local copies, waits for them, and re-layouts: 10.9 us -> 0.01 us
    ppermute x0 -> x6, starting transfers between devices: none -> 8.99 us  [swapped(): lax.ppermute(x, 'study', [(i, partner(i, k)) for i in range(count)])]
    all_to_all x1 -> x0, starting transfers between devices: 7.88 us -> none  [on_device(): gathered = lax.all_to_all(copies, 'study', 0, 0, tiled=True)]
    pallas_call x6, Pallas kernels: 19.2 us -> 15.8 us  [run(): pl.pallas_call(kernel, out_shape=out_shape, in_specs=in_specs or [VMEM_SP...]
    ppermute x0 -> x6, waiting for transfers between devices: none -> 2.25 us  [swapped(): lax.ppermute(x, 'study', [(i, partner(i, k)) for i in range(count)])]
    slice x1 -> x0, local copies, waits for them, and re-layouts: 0.72 us -> none  [on_device(): copies[:1]]
    broadcast_in_dim x1 -> x2, other arithmetic: 0.03 us -> 0.75 us  [the longest x1 0.67 us: on_device(): return jnp.swapaxes(own_part + out, 0, 1)[None]]
    broadcast_in_dim x1, local copies, waits for them, and re-layouts: 0.77 us -> 0.07 us  [on_device(): jnp.broadcast_to(jnp.stack([study_valid_length.astype(f32), study_penalty...]
  transfers between devices with their start and end apart: 4 -> 9, of which waited for: 1 -> 3; matrix products, arithmetic and copies ran while one was open for 2% -> 0% of each run, Pallas kernels for 25% -> 48%
where the time goes in v1:
time: 30.1 us; the launch traced here: 29.9 us
  Pallas kernels  15.8 us (52%)
  starting transfers between devices  9.57 us (32%)
  waiting for transfers between devices  2.27 us (8%)
  between operations  1.39 us (5%)
  other arithmetic  0.76 us (3%)
    pallas_call x6, Pallas kernels, run(): pl.pallas_call(kernel, out_shape=out_shape, in_specs=in_specs or [VMEM_SP...  15.8 us
    ppermute x6, starting transfers between devices, swapped(): lax.ppermute(x, 'study', [(i, partner(i, k)) for i in range(count)])  8.99 us
    ppermute x6, waiting for transfers between devices, swapped(): lax.ppermute(x, 'study', [(i, partner(i, k)) for i in range(count)])  2.25 us
    broadcast_in_dim x1, other arithmetic, on_device(): return jnp.swapaxes(own_part + out, 0, 1)[None]  0.67 us
  transfers between devices with their start and end apart: 9, of which 3 were waited for; matrix products, arithmetic and copies ran while one was open for 0% of the time, Pallas kernels for 48%

profile of v1, /device:TPU:0, one launch (start us, length us, event | category | flops | bytes accessed | tf_op | source)
XLA Modules:
  0.0 29.9 jit_solution(14312810816472261093)
XLA Ops:
  0.0 0.5 %collective-permute-start.4 = (s32[1,512]{1,0:T(1,128)}, s32[1,512]{1,0:T(1,128)S(1)}, u32[]{:S(2)}, u32[]{:S(2)}) collective-permute-start(s32[1,512]{1,0:T(1,128)} %refs_2_.1), channel_id=1, source_target_pairs={{1,0},{0,1},{3,2},{2,3},{5,4},{4,5},{7,6},{6,7},{9,8},{8,9},{11,10... | collective-permute-start | bytes 6152 | tf_op jit(solution)/shard_map/ppermute | solution.py:247
  0.5 0.1 collective-permute-start
  1.8 0.1 maximum_bitcast_fusion
  1.9 0.1 broadcast_in_dim.11.const_ref
  2.0 1.6 %setup.1 = (bf16[256,4096]{1,0:T(8,128)(2,1)S(1)}, bf16[64,4096]{1,0:T(8,128)(2,1)S(1)}, bf16[64,512]{1,0:T(8,128)(2,1)S(1)}, bf16[512,256]{1,0:T(8,128)(2,1)S(1)}) custom-call(f32[2,128]{1,0:T(2,128)S(1)} %broadcast_in_dim.11.const_ref, bf16[64,8192]{1,0:T(8,128)(2,1)} %freq_hbm.1, f32[1,8192]{1,0:T(1,128)} %bitcast.15, bf16[64,512]{1,0:T(8,128)(2,1)} %bitcast.14), custom_call_target="tpu_custom_call" | custom-call | flops 5242880 | bytes 1048576 | tf_op jit(solution)/shard_map/setup/pallas_call | solution.py:229
  3.5 0.0 copy-start
  3.5 6.4 %cosine_sums.1 = (f32[512,4096]{1,0:T(8,128)S(1)}, f32[512,4096]{1,0:T(8,128)S(1)}, f32[8,512]{1,0:T(8,128)S(1)}) custom-call(f32[2,128]{1,0:T(2,128)S(1)} %broadcast_in_dim.11.const_ref, bf16[256,4096]{1,0:T(8,128)(2,1)S(1)} %get-tuple-element.20.w_ref, bf16[512,256]{1,0:T(8,128)(2,1)S(1)} %get-tuple-element.21.x_own_ref, ...), custom_call_target="tpu_custom_call" | custom-call | flops 2197815296 | bytes 2097152 | tf_op jit(solution)/shard_map/cosine_sums/pallas_call | solution.py:229
  10.0 4.0 %collective-permute-start.3 = (f32[8,512]{1,0:T(8,128)S(1)}, f32[8,512]{1,0:T(8,128)S(1)}, u32[]{:S(2)}, u32[]{:S(2)}) collective-permute-start(f32[8,512]{1,0:T(8,128)S(1)} %get-tuple-element.22.mean_ref), channel_id=1, source_target_pairs={{0,6},{2,4},{4,2},{6,0},{8,14},{10,12},{12,10},{14,8},{16,22},{18,... | collective-permute-start | bytes 49160 | tf_op jit(solution)/shard_map/ppermute | solution.py:268
  14.0 0.5 %collective-permute-start.2 = (f32[8,512]{1,0:T(8,128)S(1)}, f32[8,512]{1,0:T(8,128)S(1)}, u32[]{:S(2)}, u32[]{:S(2)}) collective-permute-start(f32[8,512]{1,0:T(8,128)S(1)} %get-tuple-element.22.mean_ref), channel_id=1, source_target_pairs={{0,4},{2,6},{4,0},{6,2},{8,12},{10,14},{12,8},{14,10},{16,20},{18,... | collective-permute-start | bytes 49160 | tf_op jit(solution)/shard_map/ppermute | solution.py:268
  14.5 0.1 collective-permute-start.1
  14.6 2.0 %coupling.1.base_ref = f32[64,512]{1,0:T(8,128)S(1)} custom-call(f32[2,128]{1,0:T(2,128)S(1)} %broadcast_in_dim.11.const_ref, bf16[64,512]{1,0:T(8,128)(2,1)S(1)} %get-tuple-element.23.refs_0_, bf16[64,512]{1,0:T(8,128)(2,1)S(1)} %collective-permute-done.refs_0_.refs_1_, s32[1,512]{1,0:T(1,128)S(1)} %copy-done, s32[1,512]{1,0:T(1,128)S(1)} %collective-permute-done.4.refs_3_), custom_call_target="tpu_custom_call" | custom-call | flops 201326592 | bytes 131072 | tf_op jit(solution)/shard_map/coupling/pallas_call | solution.py:229
  16.6 0.0 collective-permute-done.3
  16.6 1.1 %collective-permute-done.2 = f32[8,512]{1,0:T(8,128)S(1)} collective-permute-done((f32[8,512]{1,0:T(8,128)S(1)}, f32[8,512]{1,0:T(8,128)S(1)}, u32[]{:S(2)}, u32[]{:S(2)}) %collective-permute-start.2) | collective-permute-done | bytes 16416 | tf_op jit(solution)/shard_map/ppermute | solution.py:268
  17.7 0.5 %collective-permute-done.1 = f32[8,512]{1,0:T(8,128)S(1)} collective-permute-done((f32[8,512]{1,0:T(8,128)S(1)}, f32[8,512]{1,0:T(8,128)S(1)}, u32[]{:S(2)}, u32[]{:S(2)}) %collective-permute-start.1) | collective-permute-done | bytes 16416 | tf_op jit(solution)/shard_map/ppermute | solution.py:268
  18.2 3.6 %collective-permute-start.7 = (f32[8,512]{1,0:T(8,128)S(1)}, f32[8,512]{1,0:T(8,128)S(1)}, u32[]{:S(2)}, u32[]{:S(2)}) collective-permute-start(f32[8,512]{1,0:T(8,128)S(1)} %add_add_fusion.1), channel_id=1, source_target_pairs={{0,24},{2,26},{4,28},{6,30},{8,16},{10,18},{12,20},{14,22},{16,8},... | collective-permute-start | bytes 49160 | tf_op jit(solution)/shard_map/ppermute | solution.py:268
  21.8 0.0 collective-permute-start.6
  21.8 0.8 %collective-permute-start.5 = (f32[8,512]{1,0:T(8,128)S(1)}, f32[8,512]{1,0:T(8,128)S(1)}, u32[]{:S(2)}, u32[]{:S(2)}) collective-permute-start(f32[8,512]{1,0:T(8,128)S(1)} %add_add_fusion.1), channel_id=1, source_target_pairs={{0,8},{2,10},{4,12},{6,14},{8,0},{10,2},{12,4},{14,6},{16,24},{18,... | collective-permute-start | bytes 49160 | tf_op jit(solution)/shard_map/ppermute | solution.py:268
  22.6 3.2 %sines.1 = (bf16[512,4096]{1,0:T(8,128)(2,1)S(1)}, bf16[512,4096]{1,0:T(8,128)(2,1)S(1)}) custom-call(f32[512,4096]{1,0:T(8,128)S(1)} %get-tuple-element.26.refs_0_, f32[512,4096]{1,0:T(8,128)S(1)} %get-tuple-element.27.refs_1_), custom_call_target="tpu_custom_call" | custom-call | flops 50331648 | bytes 25165824 | tf_op jit(solution)/shard_map/sines/pallas_call | solution.py:229
  25.8 0.7 %collective-permute-done.6 = f32[8,512]{1,0:T(8,128)S(1)} collective-permute-done((f32[8,512]{1,0:T(8,128)S(1)}, f32[8,512]{1,0:T(8,128)S(1)}, u32[]{:S(2)}, u32[]{:S(2)}) %collective-permute-start.6) | collective-permute-done | bytes 16416 | tf_op jit(solution)/shard_map/ppermute | solution.py:268
  26.5 1.3 %residual_part.1 = (f32[64,512]{1,0:T(8,128)S(1)}, bf16[128,4096]{1,0:T(8,128)(2,1)S(1)}) custom-call(f32[2,128]{1,0:T(2,128)S(1)} %broadcast_in_dim.11.const_ref, f32[8,512]{1,0:T(8,128)S(1)} %add_add_fusion.sum_ref, f32[8,512]{1,0:T(8,128)S(1)} %get-tuple-element.22.mean_ref, bf16[64,4096]{1,0:T(8,128)(2,1)S(1)} %get-tuple-element.30.freq_ref, ...), custom_call_target="tpu_custom_call" | custom-call | flops 268435456 | bytes 4194304 | tf_op jit(solution)/shard_map/residual_part/pallas_call | solution.py:229
  27.8 0.1 collective-permute-start.8
  27.9 1.3 %own_part.1 = f32[64,512]{1,0:T(8,128)S(1)} custom-call(f32[2,128]{1,0:T(2,128)S(1)} %broadcast_in_dim.11.const_ref, bf16[512,4096]{1,0:T(8,128)(2,1)S(1)} %get-tuple-element.28.s_ref, bf16[128,4096]{1,0:T(8,128)(2,1)S(1)} %get-tuple-element.32.rf_ref, f32[64,512]{1,0:T(8,128)S(1)} %coupling.1.base_ref), custom_call_target="tpu_custom_call" | custom-call | flops 268435456 | bytes 4194304 | tf_op jit(solution)/shard_map/own_part/pallas_call | solution.py:229
  29.2 0.0 collective-permute-done.8
  29.2 0.7 %add_bitcast_fusion = f32[1,512,64]{1,2,0:T(8,128)} fusion(f32[64,512]{1,0:T(8,128)S(1)} %own_part.1, f32[64,512]{1,0:T(8,128)S(1)} %collective-permute-done.8), kind=kLoop, calls=%fused_computation | loop fusion | flops 32768 | bytes 393216 | tf_op jit(solution)/shard_map/broadcast_in_dim | solution.py:372
  (7 shorter events, 0.0 us)
Async XLA Ops:
  0.0 14.6 %collective-permute-start.4 = (s32[1,512]{1,0:T(1,128)}, s32[1,512]{1,0:T(1,128)S(1)}, u32[]{:S(2)}, u32[]{:S(2)}) collective-permute-start(s32[1,512]{1,0:T(1,128)} %refs_2_.1), channel_id=1, source_target_pairs={{1,0},{0,1},{3,2},{2,3},{5,4},{4,5},{7,6},{6,7},{9,8},{8,9},{11,10... | collective-permute-start | bytes 6152 | tf_op jit(solution)/shard_map/ppermute | solution.py:247
  0.5 3.1 %collective-permute-start = (bf16[64,512]{1,0:T(8,128)(2,1)}, bf16[64,512]{1,0:T(8,128)(2,1)S(1)}, u32[]{:S(2)}, u32[]{:S(2)}) collective-permute-start(bf16[64,512]{1,0:T(8,128)(2,1)} %bitcast.13), channel_id=1, source_target_pairs={{1,0},{0,1},{3,2},{2,3},{5,4},{4,5},{7,6},{6,7},{9,8},{8,9},{11,10... | collective-permute-start | bytes 196616 | tf_op jit(solution)/shard_map/ppermute | solution.py:247
  3.5 11.1 %copy-start = (s32[1,512]{1,0:T(1,128)S(1)}, s32[1,512]{1,0:T(1,128)}, u32[]{:S(2)}) copy-start(s32[1,512]{1,0:T(1,128)} %refs_2_.1) | copy-start | bytes 6148
  10.0 6.6 %collective-permute-start.3 = (f32[8,512]{1,0:T(8,128)S(1)}, f32[8,512]{1,0:T(8,128)S(1)}, u32[]{:S(2)}, u32[]{:S(2)}) collective-permute-start(f32[8,512]{1,0:T(8,128)S(1)} %get-tuple-element.22.mean_ref), channel_id=1, source_target_pairs={{0,6},{2,4},{4,2},{6,0},{8,14},{10,12},{12,10},{14,8},{16,22},{18,... | collective-permute-start | bytes 49160 | tf_op jit(solution)/shard_map/ppermute | solution.py:268
  14.0 3.7 %collective-permute-start.2 = (f32[8,512]{1,0:T(8,128)S(1)}, f32[8,512]{1,0:T(8,128)S(1)}, u32[]{:S(2)}, u32[]{:S(2)}) collective-permute-start(f32[8,512]{1,0:T(8,128)S(1)} %get-tuple-element.22.mean_ref), channel_id=1, source_target_pairs={{0,4},{2,6},{4,0},{6,2},{8,12},{10,14},{12,8},{14,10},{16,20},{18,... | collective-permute-start | bytes 49160 | tf_op jit(solution)/shard_map/ppermute | solution.py:268
  14.5 3.7 %collective-permute-start.1 = (f32[8,512]{1,0:T(8,128)S(1)}, f32[8,512]{1,0:T(8,128)S(1)}, u32[]{:S(2)}, u32[]{:S(2)}) collective-permute-start(f32[8,512]{1,0:T(8,128)S(1)} %get-tuple-element.22.mean_ref), channel_id=1, source_target_pairs={{0,2},{2,0},{4,6},{6,4},{8,10},{10,8},{12,14},{14,12},{16,18},{18,... | collective-permute-start | bytes 49160 | tf_op jit(solution)/shard_map/ppermute | solution.py:268
  18.2 7.5 %collective-permute-start.7 = (f32[8,512]{1,0:T(8,128)S(1)}, f32[8,512]{1,0:T(8,128)S(1)}, u32[]{:S(2)}, u32[]{:S(2)}) collective-permute-start(f32[8,512]{1,0:T(8,128)S(1)} %add_add_fusion.1), channel_id=1, source_target_pairs={{0,24},{2,26},{4,28},{6,30},{8,16},{10,18},{12,20},{14,22},{16,8},... | collective-permute-start | bytes 49160 | tf_op jit(solution)/shard_map/ppermute | solution.py:268
  21.8 4.6 %collective-permute-start.6 = (f32[8,512]{1,0:T(8,128)S(1)}, f32[8,512]{1,0:T(8,128)S(1)}, u32[]{:S(2)}, u32[]{:S(2)}) collective-permute-start(f32[8,512]{1,0:T(8,128)S(1)} %add_add_fusion.1), channel_id=1, source_target_pairs={{0,16},{2,18},{4,20},{6,22},{8,24},{10,26},{12,28},{14,30},{16,0},... | collective-permute-start | bytes 49160 | tf_op jit(solution)/shard_map/ppermute | solution.py:268
  21.8 4.6 %collective-permute-start.5 = (f32[8,512]{1,0:T(8,128)S(1)}, f32[8,512]{1,0:T(8,128)S(1)}, u32[]{:S(2)}, u32[]{:S(2)}) collective-permute-start(f32[8,512]{1,0:T(8,128)S(1)} %add_add_fusion.1), channel_id=1, source_target_pairs={{0,8},{2,10},{4,12},{6,14},{8,0},{10,2},{12,4},{14,6},{16,24},{18,... | collective-permute-start | bytes 49160 | tf_op jit(solution)/shard_map/ppermute | solution.py:268
  27.8 1.4 %collective-permute-start.8 = (f32[64,512]{1,0:T(8,128)S(1)}, f32[64,512]{1,0:T(8,128)S(1)}, u32[]{:S(2)}, u32[]{:S(2)}) collective-permute-start(f32[64,512]{1,0:T(8,128)S(1)} %get-tuple-element.34), channel_id=1, source_target_pairs={{1,0},{0,1},{3,2},{2,3},{5,4},{4,5},{7,6},{6,7},{9,8},{8,9},{11,10... | collective-permute-start | bytes 393224 | tf_op jit(solution)/shard_map/ppermute | solution.py:247

commit v2 on v1

--- a/solution.py
+++ b/solution.py
@@ -20,6 +20,7 @@
 SIN_LEAD = 2.0 * COS_LEAD * abs(COS_LEAD)
 
 VMEM_SPEC = pl.BlockSpec(memory_space=pltpu.VMEM)
+SMEM_SPEC = pl.BlockSpec(memory_space=pltpu.SMEM)
 HBM_SPEC = pl.BlockSpec(memory_space=pltpu.HBM)
 
 
@@ -54,7 +55,7 @@
     x_ref[:, PAIR:] = jnp.concatenate([z, ones], axis=0).T.astype(jnp.bfloat16)
 
 
-def setup_kernel(const_ref, freq_hbm, phase_hbm, z_hbm, w_ref, freq_ref, z_ref, x_ref, phase_buf, sems):
+def setup_kernel(length_ref, freq_hbm, phase_hbm, z_hbm, w_ref, freq_ref, z_ref, x_ref, const_ref, phase_buf, sems):
     depth, width = freq_ref.shape
     start = pl.multiple_of(lax.axis_index("cell") * width, BLOCK)
     copies = [
@@ -69,8 +70,9 @@
     ]
     for copy in copies:
         copy.start()
+    length = jnp.full((1, 1), length_ref[0], jnp.int32).astype(jnp.float32)
+    const_ref[...] = jnp.broadcast_to(length, const_ref.shape)
     copies[0].wait()
-    length = const_ref[0:1, 0:1]
     store_rows(x_ref, z_ref[...], valid_row(0, z_ref.shape[1], length))
     for copy in copies[1:]:
         copy.wait()
@@ -125,68 +127,91 @@
             out_ref[:, here] = (s * (rest * lax.rsqrt(rest))).astype(jnp.bfloat16)
 
 
-def coupling_kernel(blocks, const_ref, *refs):
-    z_refs, donor_refs, out_ref = refs[:blocks], refs[blocks : 2 * blocks], refs[2 * blocks]
-    depth, cells = out_ref.shape
+def stacked(rows, cells):
+    index = lax.broadcasted_iota(jnp.int32, (DONOR_LABELS, cells), 0)
+    total = jnp.zeros((DONOR_LABELS, cells), jnp.float32)
+    for k, row in enumerate(rows):
+        if row is not None:
+            total = jnp.where(index == k, row, total)
+    return total.astype(jnp.bfloat16)
+
+
+def coupling_kernel(blocks, owner, weight_ref, const_ref, *refs):
+    z_refs, donor_refs, out_refs = refs[:blocks], refs[blocks : 2 * blocks], refs[2 * blocks :]
+    depth, cells = out_refs[0].shape
     window = blocks * cells
-    length = const_ref[0:1, 0:1]
-    weight = const_ref[1:2, 0:1]
-    inverse_n = 1.0 / length
-    label = lax.broadcasted_iota(jnp.int32, (DONOR_LABELS, cells), 0)
-    members, valids = [], []
-    counts = jnp.zeros((DONOR_LABELS, 1), jnp.float32)
-    for block in range(blocks):
-        member = (donor_refs[block][...] == label).astype(jnp.float32)
-        valid = valid_row(block, cells, length)
-        counts = counts + jnp.sum(member * valid, axis=1, keepdims=True)
-        members.append(member)
-        valids.append(valid)
-    inverse = 1.0 / jnp.maximum(counts, 1.0)
-    present = jnp.sum((counts > 0.5).astype(jnp.float32), axis=0, keepdims=True)
-    row = lax.broadcasted_iota(jnp.int32, (DONOR_LABELS, cells), 0)
-    own_inverse = jnp.sum(members[0] * inverse, axis=0, keepdims=True)
-    left_same = jnp.concatenate(split3(members[0] * (weight * inverse * inverse)), axis=0)
-    bh, bm, bl = [p.astype(jnp.float32) for p in split3(-(weight * inverse_n) * own_inverse)]
-    ones = (row < 6).astype(jnp.float32)
-    left_rest = jnp.where(row == 0, bh, jnp.where(row == 1, bm, jnp.where(row == 2, bl, ones)))
-    left = jnp.concatenate([left_same, left_rest.astype(jnp.bfloat16)], axis=0)
-    own = z_refs[0][...]
-    own_wide = own.astype(jnp.float32)
-    own_sq = jnp.sum(own_wide * own_wide, axis=0, keepdims=True)
-    total = jnp.zeros((cells, PAIR), jnp.float32)
-    minor = (((1,), (1,)), ((), ()))
-    major = (((0,), (0,)), ((), ()))
-    own_column = jnp.broadcast_to(own_sq, (PAIR, cells)).T[:, 0:1]
-    for block in range(blocks):
-        member, valid = members[block], valids[block]
-        right_inverse = jnp.sum(member * inverse, axis=0, keepdims=True)
-        rest = weight * valid * inverse_n * (present * inverse_n - right_inverse)
-        ch, cm, cl = [p.astype(jnp.float32) for p in split3(rest)]
-        right_rest = jnp.where(
-            row < 3,
-            valid,
-            jnp.where(row == 3, ch, jnp.where(row == 4, cm, jnp.where(row == 5, cl, 0.0))),
-        ).astype(jnp.bfloat16)
-        same = (member * valid).astype(jnp.bfloat16)
-        right = jnp.concatenate([same, same, same, right_rest], axis=0)
-        pair_weight = lax.dot_general(left, right, major, preferred_element_type=jnp.float32)
-        z = z_refs[block][...]
-        wide = z.astype(jnp.float32)
-        right_sq = jnp.sum(wide * wide, axis=0, keepdims=True)
-        inner = lax.dot_general(own, z, major, preferred_element_type=jnp.float32)
-        squared = own_column + right_sq - 2.0 * inner
-        coupling = pair_weight * jnp.exp(squared * (-0.5 / depth))
-        hi = coupling.astype(jnp.bfloat16)
-        low = (coupling - hi.astype(jnp.float32)).astype(jnp.bfloat16)
-        right_rows = jnp.concatenate([z, jnp.ones((PAIR - depth, cells), jnp.bfloat16)], axis=0)
-        for part in (hi, low):
-            total = total + lax.dot_general(
-                part, right_rows, minor, preferred_element_type=jnp.float32
+    f32, bf16 = jnp.float32, jnp.bfloat16
+
+    def compute():
+        length = const_ref[0:1, 0:1]
+        inverse_n = 1.0 / length
+        label = lax.broadcasted_iota(jnp.int32, (DONOR_LABELS, cells), 0)
+        members = [(ref[...] == label).astype(f32) for ref in donor_refs]
+        valids = [valid_row(block, cells, length) for block in range(blocks)]
+        counts = sum(
+            jnp.sum(member * valid, axis=1, keepdims=True)
+            for member, valid in zip(members, valids)
+        )
+        inverse = 1.0 / jnp.maximum(counts, 1.0)
+        present = jnp.sum((counts > 0.5).astype(f32), axis=0, keepdims=True)
+        one = jnp.ones((1, 1), f32)
+        wides = [ref[...].astype(f32) for ref in z_refs]
+        norms = [
+            [p.astype(f32) for p in split3(-0.5 * jnp.sum(z * z, axis=0, keepdims=True))]
+            for z in wides
+        ]
+        shares = [
+            inverse_n * jnp.sum(member * inverse, axis=0, keepdims=True) for member in members
+        ]
+        same_zero = jnp.zeros((3 * DONOR_LABELS, cells), bf16)
+        z_zero = jnp.zeros((depth, cells), bf16)
+        rights = []
+        for target in range(len(out_refs)):
+            rest = [p.astype(f32) for p in split3(present * inverse_n * inverse_n - shares[target])]
+            member = members[target].astype(bf16)
+            exponent = [z_refs[target][...], stacked([one] * 3 + norms[target], cells), same_zero]
+            pair = [z_zero, stacked([None] * 6 + [one] * 3 + rest, cells), member, member, member]
+            rights.append(
+                jnp.concatenate(
+                    [jnp.concatenate(exponent, axis=0), jnp.concatenate(pair, axis=0)], axis=1
+                )
             )
-    total = total.T
-    scale = -(2.0 * window / depth)
-    own_valid = valid_row(0, cells, length)
-    out_ref[...] = scale * own_valid * (own_wide * total[depth : depth + 1] - total[:depth])
+        totals = [jnp.zeros((PAIR, cells), f32) for _ in out_refs]
+        for source in range(blocks):
+            valid = valids[source]
+            z = z_refs[source][...]
+            minus = [p.astype(f32) for p in split3(-shares[source] * valid)]
+            left = jnp.concatenate(
+                [
+                    z,
+                    stacked(norms[source] + [one] * 3 + minus + [valid] * 3, cells),
+                    *split3(members[source] * (inverse * inverse) * valid),
+                ],
+                axis=0,
+            ).astype(f32).T.astype(bf16)
+            rows = jnp.concatenate([z, jnp.ones((PAIR - depth, cells), bf16)], axis=0)
+            for target, right in enumerate(rights):
+                both = jnp.dot(left, right, preferred_element_type=f32)
+                coupling = both[:, cells:] * jnp.exp2(both[:, :cells] * (math.log2(math.e) / depth))
+                hi = coupling.astype(bf16)
+                low = (coupling - hi.astype(f32)).astype(bf16)
+                totals[target] += jnp.dot(rows, hi, preferred_element_type=f32)
+                totals[target] += jnp.dot(rows, low, preferred_element_type=f32)
+        scale = -(2.0 * window / depth) * jnp.full((1, 1), weight_ref[0], f32)
+        for target, out_ref in enumerate(out_refs):
+            total = totals[target]
+            gradient = wides[target] * total[depth : depth + 1] - total[:depth]
+            out_ref[...] = scale * valids[target] * gradient
+
+    if owner is None:
+        compute()
+        return
+    pl.when(lax.axis_index("cell") == owner)(compute)
+
+    @pl.when(lax.axis_index("cell") != owner)
+    def _():
+        for out_ref in out_refs:
+            out_ref[...] = jnp.zeros((depth, cells), f32)
 
 
 def feature_part(block, const_ref, s_ref, rf_ref, window):
@@ -200,7 +225,8 @@
     return factor * valid_row(block, cells, length) * (both[:depth] + both[depth:])
 
 
-def residual_kernel(block, window, const_ref, sum_ref, mean_ref, freq_ref, s_ref, out_ref, rf_ref):
+def residual_kernel(block, window, const_ref, sum_ref, mean_ref, freq_ref, s_ref, *refs):
+    *base_refs, out_ref, rf_ref = refs
     strip = sum_ref.shape[1]
     depth = freq_ref.shape[0]
     center = sum_ref[...] * (1.0 / lax.axis_size("study"))
@@ -211,15 +237,13 @@
         hi = rows.astype(jnp.bfloat16)
         rf_ref[:depth, here] = hi
         rf_ref[depth:, here] = (rows - hi.astype(jnp.float32)).astype(jnp.bfloat16)
-    out_ref[...] = feature_part(block, const_ref, s_ref, rf_ref, window)
-
-
-def other_kernel(block, window, const_ref, s_ref, rf_ref, out_ref):
-    out_ref[...] = feature_part(block, const_ref, s_ref, rf_ref, window)
-
-
-def own_kernel(window, const_ref, s_ref, rf_ref, base_ref, out_ref):
-    out_ref[...] = base_ref[...] + feature_part(0, const_ref, s_ref, rf_ref, window)
+    part_kernel(block, window, const_ref, s_ref, rf_ref, *base_refs, out_ref)
+
+
+def part_kernel(block, window, const_ref, s_ref, rf_ref, *refs):
+    *base_refs, out_ref = refs
+    part = feature_part(block, const_ref, s_ref, rf_ref, window)
+    out_ref[...] = sum((ref[...] for ref in base_refs), part)
 
 
 def call(kernel, out_shape, name, flops, transcendentals=0, size=0, scratch=(), vmem=8, in_specs=None):
@@ -242,6 +266,10 @@
     return run
 
 
+def in_hbm(x):
+    return pltpu.with_memory_space_constraint(x, pltpu.HBM)
+
+
 def rotated(x, shift):
     count = lax.axis_size("cell")
     return lax.ppermute(x, "cell", [((i + shift) % count, i) for i in range(count)])
@@ -266,7 +294,7 @@
 
     return [
         lax.ppermute(x, "study", [(i, partner(i, k)) for i in range(count)])
-        for k in range(1, radix)
+        for k in range(radix - 1, 0, -1)
     ]
 
 
@@ -286,27 +314,24 @@
     others = [rotated(own, k) for k in range(1, blocks)]
     donors = [donor_ids] + [rotated(donor_ids, k) for k in range(1, blocks)]
 
-    consts = jnp.broadcast_to(
-        jnp.stack([study_valid_length.astype(f32), study_penalty_weight]), (2, 128)
-    )
-    in_hbm = [
-        pltpu.with_memory_space_constraint(operand, pltpu.HBM)
-        for operand in (frequencies, phases.reshape(1, features), own)
-    ]
-    turn_weights, freq_part, own, x_own = call(
+    turn_weights, freq_part, own, x_own, consts = call(
         setup_kernel,
         [
             shape((2 * PAIR, width), bf16),
             shape((depth, width), bf16),
             shape((depth, cells), bf16),
             shape((cells, 2 * PAIR), bf16),
+            shape((1, 128), f32),
         ],
         "setup",
         flops=20 * depth * width,
         size=4 * depth * width,
         scratch=[pltpu.VMEM((1, width), f32), pltpu.SemaphoreType.DMA((3,))],
-        in_specs=[VMEM_SPEC] + [HBM_SPEC] * 3,
-    )(consts, *in_hbm)
+        in_specs=[SMEM_SPEC] + [HBM_SPEC] * 3,
+    )(
+        study_valid_length,
+        *[in_hbm(x) for x in (frequencies, phases.reshape(1, features), own)],
+    )
 
     *halves, mean = call(
         functools.partial(cosine_kernel, blocks),
@@ -317,57 +342,62 @@
         scratch=[pltpu.VMEM((cells, 2 * PAIR), bf16)] * (blocks - 1),
     )(consts, turn_weights, x_own, *others)
 
-    def couplings(z_blocks):
+    def couplings():
+        outputs, owner = (2, 1) if blocks == 2 else (1, None)
         return call(
-            functools.partial(coupling_kernel, blocks),
-            shape((depth, cells), f32),
+            functools.partial(coupling_kernel, blocks, owner),
+            [shape((depth, cells), f32)] * outputs,
             "coupling",
             flops=2 * cells * window * (3 * depth),
             transcendentals=cells * window,
             size=4 * cells * depth,
-        )(consts, *z_blocks, *donors)
-
-    center, base, stride = mean, None, 1
-    for radix in digits(studies):
+            in_specs=[SMEM_SPEC] + [VMEM_SPEC] * (1 + 2 * blocks),
+        )(study_penalty_weight, consts, own, *others, *donors)
+
+    def sine_parts(halves):
+        return call(
+            functools.partial(sine_kernel, len(halves)),
+            [shape((cells, width), bf16)] * len(halves),
+            "sines",
+            flops=12 * pairs,
+            transcendentals=pairs,
+            size=6 * pairs,
+        )(*halves)
+
+    study_penalty_weight, mean = lax.optimization_barrier((study_penalty_weight, mean))
+    center, stride, beside = mean, 1, []
+    for turn, radix in enumerate(digits(studies)):
         parts = swapped(center, stride, radix)
         stride *= radix
-        if base is None:
-            base = couplings([own, *others])
-            center = sum(parts, center)
-            center, base, *halves = lax.optimization_barrier((center, base, *halves))
-        else:
-            center = sum(parts, center)
-    if base is None:
-        base = couplings([own, *others])
-
-    sines = call(
-        functools.partial(sine_kernel, blocks),
-        [shape((cells, width), bf16)] * blocks,
-        "sines",
-        flops=12 * pairs,
-        transcendentals=pairs,
-        size=6 * pairs,
-    )(*halves)
+        if turn == 0:
+            bases, sines = couplings(), sine_parts(halves[1:])
+            beside = [*bases, *sines, *halves[:1]]
+        elif turn == 1:
+            sines = [*sine_parts(beside[-1:]), *beside[len(bases) : -1]]
+            beside = [*beside[: len(bases)], *sines]
+        center, *beside = lax.optimization_barrier((sum(parts, center), *beside))
+    bases, sines = beside[: len(bases)], beside[len(bases) :]
 
     out, residual_freq = None, None
     part_shape = shape((depth, cells), f32)
     cost = dict(flops=2 * cells * width * depth, size=2 * cells * width)
     for block in range(1, blocks):
+        base = bases[block : block + 1]
         if residual_freq is None:
             part, residual_freq = call(
                 functools.partial(residual_kernel, block, window),
                 [part_shape, shape((2 * depth, width), bf16)],
                 "residual_part",
                 **cost,
-            )(consts, center, mean, freq_part, sines[block])
+            )(consts, center, mean, freq_part, sines[block], *base)
         else:
             part = call(
-                functools.partial(other_kernel, block, window), part_shape, "other_part", **cost
-            )(consts, sines[block], residual_freq)
+                functools.partial(part_kernel, block, window), part_shape, "other_part", **cost
+            )(consts, sines[block], residual_freq, *base)
         sent = rotated(part, blocks - block)
         out = sent if out is None else out + sent
-    own_part = call(functools.partial(own_kernel, window), part_shape, "own_part", **cost)(
-        consts, sines[0], residual_freq, base
+    own_part = call(functools.partial(part_kernel, 0, window), part_shape, "own_part", **cost)(
+        consts, sines[0], residual_freq, bases[0]
     )
     return jnp.swapaxes(own_part + out, 0, 1)[None]
 

time: 30.1 us -> 29.9 us (level)
  waiting for transfers between devices: 2.27 us -> 4.22 us
  Pallas kernels: 15.8 us -> 13.9 us
    pallas_call x6 -> x7, Pallas kernels: 15.8 us -> 13.9 us  [run(): pl.pallas_call(kernel, out_shape=out_shape, in_specs=in_specs or [VMEM_SP...]
    ppermute x6, waiting for transfers between devices: 2.25 us -> 4.2 us  [swapped(): lax.ppermute(x, 'study', [(i, partner(i, k)) for i in range(count)])]
  transfers between devices with their start and end apart: 9 -> 9, of which waited for: 3 -> 3; matrix products, arithmetic and copies ran while one was open for 0% -> 0% of each run, Pallas kernels for 48% -> 42%
where the time goes in v2:
time: 29.9 us; the launch traced here: 29.7 us
  Pallas kernels  13.9 us (46%)
  starting transfers between devices  9.57 us (32%)
  waiting for transfers between devices  4.22 us (14%)
  between operations  1.4 us (5%)
  other arithmetic  0.69 us (2%)
    pallas_call x7, Pallas kernels, run(): pl.pallas_call(kernel, out_shape=out_shape, in_specs=in_specs or [VMEM_SP...  13.9 us
    ppermute x6, starting transfers between devices, swapped(): lax.ppermute(x, 'study', [(i, partner(i, k)) for i in range(count)])  8.99 us
    ppermute x6, waiting for transfers between devices, swapped(): lax.ppermute(x, 'study', [(i, partner(i, k)) for i in range(count)])  4.2 us
    broadcast_in_dim x1, other arithmetic, on_device(): return jnp.swapaxes(own_part + out, 0, 1)[None]  0.67 us
  transfers between devices with their start and end apart: 9, of which 3 were waited for; matrix products, arithmetic and copies ran while one was open for 0% of the time, Pallas kernels for 42%

profile of v2, /device:TPU:0, one launch (start us, length us, event | category | flops | bytes accessed | tf_op | source)
XLA Modules:
  0.0 29.7 jit_solution(13110746159288458107)
XLA Ops:
  0.0 0.5 %collective-permute-start = (bf16[64,512]{1,0:T(8,128)(2,1)}, bf16[64,512]{1,0:T(8,128)(2,1)S(1)}, u32[]{:S(2)}, u32[]{:S(2)}) collective-permute-start(bf16[64,512]{1,0:T(8,128)(2,1)} %bitcast.8), channel_id=1, source_target_pairs={{1,0},{0,1},{3,2},{2,3},{5,4},{4,5},{7,6},{6,7},{9,8},{8,9},{11,10... | collective-permute-start | bytes 196616 | tf_op jit(solution)/shard_map/ppermute | solution.py:275
  0.5 0.1 collective-permute-start.4
  1.8 1.6 %setup.1 = (bf16[256,4096]{1,0:T(8,128)(2,1)S(1)}, bf16[64,4096]{1,0:T(8,128)(2,1)S(1)}, bf16[64,512]{1,0:T(8,128)(2,1)S(1)}, bf16[512,256]{1,0:T(8,128)(2,1)S(1)}, f32[1,128]{1,0:T(1,128)S(1)}) custom-call(s32[1]{0:T(128)S(6)} %copy.7.length_ref, bf16[64,8192]{1,0:T(8,128)(2,1)} %freq_hbm.1, f32[1,8192]{1,0:T(1,128)} %bitcast.10, bf16[64,512]{1,0:T(8,128)(2,1)} %bitcast.9), custom_call_target="tpu_custom_call" | custom-call | flops 5242880 | bytes 1048576 | tf_op jit(solution)/shard_map/setup/pallas_call | solution.py:253
  3.4 0.0 collective-permute-done.refs_0_.refs_1_
  3.4 6.5 %cosine_sums.1 = (f32[512,4096]{1,0:T(8,128)S(1)}, f32[512,4096]{1,0:T(8,128)S(1)}, f32[8,512]{1,0:T(8,128)S(1)}) custom-call(f32[1,128]{1,0:T(1,128)S(1)} %get-tuple-element.29.const_ref, bf16[256,4096]{1,0:T(8,128)(2,1)S(1)} %get-tuple-element.30.w_ref, bf16[512,256]{1,0:T(8,128)(2,1)S(1)} %get-tuple-element.31.x_own_ref, ...), custom_call_target="tpu_custom_call" | custom-call | flops 2197815296 | bytes 2097152 | tf_op jit(solution)/shard_map/cosine_sums/pallas_call | solution.py:253
  9.8 4.0 %collective-permute-start.1 = (f32[8,512]{1,0:T(8,128)S(1)}, f32[8,512]{1,0:T(8,128)S(1)}, u32[]{:S(2)}, u32[]{:S(2)}) collective-permute-start(f32[8,512]{1,0:T(8,128)S(1)} %get-tuple-element.33.mean_ref), channel_id=1, source_target_pairs={{0,6},{2,4},{4,2},{6,0},{8,14},{10,12},{12,10},{14,8},{16,22},{18,... | collective-permute-start | bytes 49160 | tf_op jit(solution)/shard_map/ppermute | solution.py:296
  13.8 0.5 %collective-permute-start.2 = (f32[8,512]{1,0:T(8,128)S(1)}, f32[8,512]{1,0:T(8,128)S(1)}, u32[]{:S(2)}, u32[]{:S(2)}) collective-permute-start(f32[8,512]{1,0:T(8,128)S(1)} %get-tuple-element.33.mean_ref), channel_id=1, source_target_pairs={{0,4},{2,6},{4,0},{6,2},{8,12},{10,14},{12,8},{14,10},{16,20},{18,... | collective-permute-start | bytes 49160 | tf_op jit(solution)/shard_map/ppermute | solution.py:296
  14.3 0.1 collective-permute-start.3
  14.4 1.5 %sines.2.s_ref = bf16[512,4096]{1,0:T(8,128)(2,1)S(1)} custom-call(f32[512,4096]{1,0:T(8,128)S(1)} %get-tuple-element.38.refs_0_), custom_call_target="tpu_custom_call" | custom-call | flops 50331648 | bytes 25165824 | tf_op jit(solution)/shard_map/sines/pallas_call | solution.py:253
  15.9 0.0 collective-permute-done.4.refs_3_
  16.0 0.2 coupling.1
  16.2 0.0 collective-permute-done.1
  16.2 1.3 %collective-permute-done.2 = f32[8,512]{1,0:T(8,128)S(1)} collective-permute-done((f32[8,512]{1,0:T(8,128)S(1)}, f32[8,512]{1,0:T(8,128)S(1)}, u32[]{:S(2)}, u32[]{:S(2)}) %collective-permute-start.2) | collective-permute-done | bytes 16416 | tf_op jit(solution)/shard_map/ppermute | solution.py:296
  17.5 0.5 %collective-permute-done.3 = f32[8,512]{1,0:T(8,128)S(1)} collective-permute-done((f32[8,512]{1,0:T(8,128)S(1)}, f32[8,512]{1,0:T(8,128)S(1)}, u32[]{:S(2)}, u32[]{:S(2)}) %collective-permute-start.3) | collective-permute-done | bytes 16416 | tf_op jit(solution)/shard_map/ppermute | solution.py:296
  18.1 3.6 %collective-permute-start.5 = (f32[8,512]{1,0:T(8,128)S(1)}, f32[8,512]{1,0:T(8,128)S(1)}, u32[]{:S(2)}, u32[]{:S(2)}) collective-permute-start(f32[8,512]{1,0:T(8,128)S(1)} %add_add_fusion.1), channel_id=1, source_target_pairs={{0,24},{2,26},{4,28},{6,30},{8,16},{10,18},{12,20},{14,22},{16,8},... | collective-permute-start | bytes 49160 | tf_op jit(solution)/shard_map/ppermute | solution.py:296
  21.7 0.8 %collective-permute-start.7 = (f32[8,512]{1,0:T(8,128)S(1)}, f32[8,512]{1,0:T(8,128)S(1)}, u32[]{:S(2)}, u32[]{:S(2)}) collective-permute-start(f32[8,512]{1,0:T(8,128)S(1)} %add_add_fusion.1), channel_id=1, source_target_pairs={{0,8},{2,10},{4,12},{6,14},{8,0},{10,2},{12,4},{14,6},{16,24},{18,... | collective-permute-start | bytes 49160 | tf_op jit(solution)/shard_map/ppermute | solution.py:296
  22.4 1.5 %sines.3.s_ref = bf16[512,4096]{1,0:T(8,128)(2,1)S(1)} custom-call(f32[512,4096]{1,0:T(8,128)S(1)} %get-tuple-element.43.refs_0_), custom_call_target="tpu_custom_call" | custom-call | flops 50331648 | bytes 25165824 | tf_op jit(solution)/shard_map/sines/pallas_call | solution.py:253
  23.9 0.0 collective-permute-done.5
  24.0 2.3 %collective-permute-done.6 = f32[8,512]{1,0:T(8,128)S(1)} collective-permute-done((f32[8,512]{1,0:T(8,128)S(1)}, f32[8,512]{1,0:T(8,128)S(1)}, u32[]{:S(2)}, u32[]{:S(2)}) %collective-permute-start.6) | collective-permute-done | bytes 16416 | tf_op jit(solution)/shard_map/ppermute | solution.py:296
  26.3 1.3 %residual_part.1 = (f32[64,512]{1,0:T(8,128)S(1)}, bf16[128,4096]{1,0:T(8,128)(2,1)S(1)}) custom-call(f32[1,128]{1,0:T(1,128)S(1)} %get-tuple-element.29.const_ref, f32[8,512]{1,0:T(8,128)S(1)} %add_add_fusion.sum_ref, f32[8,512]{1,0:T(8,128)S(1)} %get-tuple-element.33.mean_ref, bf16[64,4096]{1,0:T(8,128)(2,1)S(1)} %get-tuple-element.47.freq_ref, ...), custom_call_target="tpu_custom_call" | custom-call | flops 268435456 | bytes 4194304 | tf_op jit(solution)/shard_map/residual_part/pallas_call | solution.py:253
  27.6 0.1 collective-permute-start.8
  27.7 1.3 %own_part.1 = f32[64,512]{1,0:T(8,128)S(1)} custom-call(f32[1,128]{1,0:T(1,128)S(1)} %get-tuple-element.29.const_ref, bf16[512,4096]{1,0:T(8,128)(2,1)S(1)} %sines.3.s_ref, bf16[128,4096]{1,0:T(8,128)(2,1)S(1)} %get-tuple-element.50.rf_ref, f32[64,512]{1,0:T(8,128)S(1)} %get-tuple-element.51.refs_0_), custom_call_target="tpu_custom_call" | custom-call | flops 268435456 | bytes 4194304 | tf_op jit(solution)/shard_map/own_part/pallas_call | solution.py:253
  29.0 0.0 collective-permute-done.8
  29.1 0.7 %add_bitcast_fusion = f32[1,512,64]{1,2,0:T(8,128)} fusion(f32[64,512]{1,0:T(8,128)S(1)} %own_part.1, f32[64,512]{1,0:T(8,128)S(1)} %collective-permute-done.8), kind=kLoop, calls=%fused_computation | loop fusion | flops 32768 | bytes 393216 | tf_op jit(solution)/shard_map/broadcast_in_dim | solution.py:402
  (6 shorter events, 0.0 us)
Async XLA Ops:
  0.0 3.4 %collective-permute-start = (bf16[64,512]{1,0:T(8,128)(2,1)}, bf16[64,512]{1,0:T(8,128)(2,1)S(1)}, u32[]{:S(2)}, u32[]{:S(2)}) collective-permute-start(bf16[64,512]{1,0:T(8,128)(2,1)} %bitcast.8), channel_id=1, source_target_pairs={{1,0},{0,1},{3,2},{2,3},{5,4},{4,5},{7,6},{6,7},{9,8},{8,9},{11,10... | collective-permute-start | bytes 196616 | tf_op jit(solution)/shard_map/ppermute | solution.py:275
  0.5 15.5 %collective-permute-start.4 = (s32[1,512]{1,0:T(1,128)}, s32[1,512]{1,0:T(1,128)S(1)}, u32[]{:S(2)}, u32[]{:S(2)}) collective-permute-start(s32[1,512]{1,0:T(1,128)} %refs_2_.1), channel_id=1, source_target_pairs={{1,0},{0,1},{3,2},{2,3},{5,4},{4,5},{7,6},{6,7},{9,8},{8,9},{11,10... | collective-permute-start | bytes 6152 | tf_op jit(solution)/shard_map/ppermute | solution.py:275
  9.8 6.3 %collective-permute-start.1 = (f32[8,512]{1,0:T(8,128)S(1)}, f32[8,512]{1,0:T(8,128)S(1)}, u32[]{:S(2)}, u32[]{:S(2)}) collective-permute-start(f32[8,512]{1,0:T(8,128)S(1)} %get-tuple-element.33.mean_ref), channel_id=1, source_target_pairs={{0,6},{2,4},{4,2},{6,0},{8,14},{10,12},{12,10},{14,8},{16,22},{18,... | collective-permute-start | bytes 49160 | tf_op jit(solution)/shard_map/ppermute | solution.py:296
  13.8 3.7 %collective-permute-start.2 = (f32[8,512]{1,0:T(8,128)S(1)}, f32[8,512]{1,0:T(8,128)S(1)}, u32[]{:S(2)}, u32[]{:S(2)}) collective-permute-start(f32[8,512]{1,0:T(8,128)S(1)} %get-tuple-element.33.mean_ref), channel_id=1, source_target_pairs={{0,4},{2,6},{4,0},{6,2},{8,12},{10,14},{12,8},{14,10},{16,20},{18,... | collective-permute-start | bytes 49160 | tf_op jit(solution)/shard_map/ppermute | solution.py:296
  14.3 3.7 %collective-permute-start.3 = (f32[8,512]{1,0:T(8,128)S(1)}, f32[8,512]{1,0:T(8,128)S(1)}, u32[]{:S(2)}, u32[]{:S(2)}) collective-permute-start(f32[8,512]{1,0:T(8,128)S(1)} %get-tuple-element.33.mean_ref), channel_id=1, source_target_pairs={{0,2},{2,0},{4,6},{6,4},{8,10},{10,8},{12,14},{14,12},{16,18},{18,... | collective-permute-start | bytes 49160 | tf_op jit(solution)/shard_map/ppermute | solution.py:296
  14.4 1.5 %copy-start = (s32[1,512]{1,0:T(1,128)S(1)}, s32[1,512]{1,0:T(1,128)}, u32[]{:S(2)}) copy-start(s32[1,512]{1,0:T(1,128)} %refs_2_.1) | copy-start | bytes 6148
  18.1 5.9 %collective-permute-start.5 = (f32[8,512]{1,0:T(8,128)S(1)}, f32[8,512]{1,0:T(8,128)S(1)}, u32[]{:S(2)}, u32[]{:S(2)}) collective-permute-start(f32[8,512]{1,0:T(8,128)S(1)} %add_add_fusion.1), channel_id=1, source_target_pairs={{0,24},{2,26},{4,28},{6,30},{8,16},{10,18},{12,20},{14,22},{16,8},... | collective-permute-start | bytes 49160 | tf_op jit(solution)/shard_map/ppermute | solution.py:296
  21.7 4.6 %collective-permute-start.6 = (f32[8,512]{1,0:T(8,128)S(1)}, f32[8,512]{1,0:T(8,128)S(1)}, u32[]{:S(2)}, u32[]{:S(2)}) collective-permute-start(f32[8,512]{1,0:T(8,128)S(1)} %add_add_fusion.1), channel_id=1, source_target_pairs={{0,16},{2,18},{4,20},{6,22},{8,24},{10,26},{12,28},{14,30},{16,0},... | collective-permute-start | bytes 49160 | tf_op jit(solution)/shard_map/ppermute | solution.py:296
  21.7 4.6 %collective-permute-start.7 = (f32[8,512]{1,0:T(8,128)S(1)}, f32[8,512]{1,0:T(8,128)S(1)}, u32[]{:S(2)}, u32[]{:S(2)}) collective-permute-start(f32[8,512]{1,0:T(8,128)S(1)} %add_add_fusion.1), channel_id=1, source_target_pairs={{0,8},{2,10},{4,12},{6,14},{8,0},{10,2},{12,4},{14,6},{16,24},{18,... | collective-permute-start | bytes 49160 | tf_op jit(solution)/shard_map/ppermute | solution.py:296
  27.6 1.4 %collective-permute-start.8 = (f32[64,512]{1,0:T(8,128)S(1)}, f32[64,512]{1,0:T(8,128)S(1)}, u32[]{:S(2)}, u32[]{:S(2)}) collective-permute-start(f32[64,512]{1,0:T(8,128)S(1)} %get-tuple-element.52), channel_id=1, source_target_pairs={{1,0},{0,1},{3,2},{2,3},{5,4},{4,5},{7,6},{6,7},{9,8},{8,9},{11,10... | collective-permute-start | bytes 393224 | tf_op jit(solution)/shard_map/ppermute | solution.py:275

commit v3 on v2

--- a/solution.py
+++ b/solution.py
@@ -10,8 +10,10 @@
 
 DONOR_LABELS = 16
 FEATURE_PENALTY = 16.0
-BLOCK = 256
+BLOCK = 1024
 PAIR = 128
+LANES = 128
+PHASE_ROWS = 16
 SUBLANES = 8
 MIB = 1 << 20
 
@@ -46,13 +48,14 @@
     return math.sqrt(2.0 / (width * lax.axis_size("cell")))
 
 
-def store_rows(x_ref, z, valid):
+def store_cells(x_ref, z, valid):
     depth, cells = z.shape
-    z = z.astype(jnp.float32) * valid
-    tail = 2 * PAIR - 3 * depth
+    z = (z.astype(jnp.float32) * valid).astype(jnp.bfloat16)
+    for part in range(3):
+        x_ref[part * depth : (part + 1) * depth, :] = z
+    tail = x_ref.shape[0] - 3 * depth
     ones = jnp.where(lax.broadcasted_iota(jnp.int32, (tail, cells), 0) < 3, valid, 0.0)
-    x_ref[:, :PAIR] = jnp.concatenate([z, z], axis=0).T.astype(jnp.bfloat16)
-    x_ref[:, PAIR:] = jnp.concatenate([z, ones], axis=0).T.astype(jnp.bfloat16)
+    x_ref[3 * depth :, :] = ones.astype(jnp.bfloat16)
 
 
 def setup_kernel(length_ref, freq_hbm, phase_hbm, z_hbm, w_ref, freq_ref, z_ref, x_ref, const_ref, phase_buf, sems):
@@ -72,18 +75,19 @@
         copy.start()
     length = jnp.full((1, 1), length_ref[0], jnp.int32).astype(jnp.float32)
     const_ref[...] = jnp.broadcast_to(length, const_ref.shape)
+    row = 3 * depth + PHASE_ROWS
+    w_ref[row:, :] = jnp.zeros((2 * PAIR - row, width), jnp.bfloat16)
     copies[0].wait()
-    store_rows(x_ref, z_ref[...], valid_row(0, z_ref.shape[1], length))
+    store_cells(x_ref, z_ref[...], valid_row(0, z_ref.shape[1], length))
     for copy in copies[1:]:
         copy.wait()
     turn = 1.0 / (2.0 * math.pi)
     for part, rows in enumerate(split3(freq_ref[...].astype(jnp.float32) * turn)):
         w_ref[part * depth : (part + 1) * depth, :] = rows
-    tail = 2 * PAIR - 3 * depth
     hi, mid, low = [p.astype(jnp.float32) for p in split3(phase_buf[...] * turn)]
-    row = lax.broadcasted_iota(jnp.int32, (tail, width), 0)
-    rows = jnp.where(row == 0, hi, jnp.where(row == 1, mid, jnp.where(row == 2, low, 0.0)))
-    w_ref[3 * depth :, :] = rows.astype(jnp.bfloat16)
+    index = lax.broadcasted_iota(jnp.int32, (PHASE_ROWS, width), 0)
+    rows = jnp.where(index == 0, hi, jnp.where(index == 1, mid, jnp.where(index == 2, low, 0.0)))
+    w_ref[3 * depth : row, :] = rows.astype(jnp.bfloat16)
 
 
 def cosine_kernel(blocks, const_ref, w_ref, x_own_ref, *refs):
@@ -91,40 +95,43 @@
     s_refs = refs[blocks - 1 : 2 * blocks - 1]
     mean_ref = refs[2 * blocks - 1]
     x_refs = [x_own_ref, *refs[2 * blocks :]]
-    cells, width = s_refs[0].shape
+    width, cells = s_refs[0].shape
     length = const_ref[0:1, 0:1]
     for block in range(1, blocks):
-        store_rows(x_refs[block], z_refs[block - 1][...], valid_row(block, cells, length))
+        store_cells(x_refs[block], z_refs[block - 1][...], valid_row(block, cells, length))
     scale = feature_scale(width)
     per_length = 1.0 / length
     a, b, c = COS_TERMS
     strip = mean_ref.shape[1]
     for offset in range(0, width, BLOCK):
         here = slice(offset, offset + BLOCK)
-        squares = jnp.zeros((SUBLANES, BLOCK), jnp.float32)
+        weights = w_ref[:, here].T
+        squares = jnp.zeros((BLOCK, LANES), jnp.float32)
         for x_ref, s_ref in zip(x_refs, s_refs):
-            t = jnp.dot(x_ref[...], w_ref[:, here], preferred_element_type=jnp.float32)
+            t = jnp.dot(weights, x_ref[...], preferred_element_type=jnp.float32)
             r = t - jnp.round(t)
             u = r * r
             s = r * (((u + a) * u + b) * u + c)
-            s_ref[:, here] = s
-            squares += jnp.sum((s * s).reshape(cells // SUBLANES, SUBLANES, BLOCK), axis=0)
-        squares = jnp.sum(squares, axis=0, keepdims=True)
+            s_ref[here, :] = s
+            for lane in range(0, cells, LANES):
+                part = s[:, lane : lane + LANES]
+                squares += part * part
+        squares = jnp.sum(squares.T, axis=0, keepdims=True)
         mean = scale - (2.0 * scale * COS_LEAD * COS_LEAD) * per_length * squares
-        for piece in range(0, BLOCK, 128):
+        for piece in range(0, BLOCK, LANES):
             row, column = divmod(offset + piece, strip)
-            mean_ref[row : row + 1, column : column + 128] = mean[:, piece : piece + 128]
+            mean_ref[row : row + 1, column : column + LANES] = mean[:, piece : piece + LANES]
 
 
 def sine_kernel(blocks, *refs):
     top = (1.0 + 2e-6) / (COS_LEAD * COS_LEAD)
-    cells, width = refs[0].shape
+    width = refs[0].shape[0]
     for s_ref, out_ref in zip(refs[:blocks], refs[blocks:]):
         for offset in range(0, width, BLOCK):
             here = slice(offset, offset + BLOCK)
-            s = s_ref[:, here]
+            s = s_ref[here, :]
             rest = top - s * s
-            out_ref[:, here] = (s * (rest * lax.rsqrt(rest))).astype(jnp.bfloat16)
+            out_ref[here, :] = (s * (rest * lax.rsqrt(rest))).astype(jnp.bfloat16)
 
 
 def stacked(rows, cells):
@@ -215,11 +222,9 @@
 
 
 def feature_part(block, const_ref, s_ref, rf_ref, window):
-    cells, width = s_ref.shape
+    width, cells = s_ref.shape
     depth = rf_ref.shape[0] // 2
-    both = lax.dot_general(
-        s_ref[...], rf_ref[...], (((1,), (1,)), ((), ())), preferred_element_type=jnp.float32
-    ).T
+    both = jnp.dot(rf_ref[...], s_ref[...], preferred_element_type=jnp.float32)
     length = const_ref[0:1, 0:1]
     factor = -(SIN_LEAD * window * feature_scale(width)) / length
     return factor * valid_row(block, cells, length) * (both[:depth] + both[depth:])
@@ -320,7 +325,7 @@
             shape((2 * PAIR, width), bf16),
             shape((depth, width), bf16),
             shape((depth, cells), bf16),
-            shape((cells, 2 * PAIR), bf16),
+            shape((2 * PAIR, cells), bf16),
             shape((1, 128), f32),
         ],
         "setup",
@@ -335,11 +340,11 @@
 
     *halves, mean = call(
         functools.partial(cosine_kernel, blocks),
-        [shape((cells, width), f32)] * blocks + [shape((SUBLANES, strip), f32)],
+        [shape((width, cells), f32)] * blocks + [shape((SUBLANES, strip), f32)],
         "cosine_sums",
         flops=4 * PAIR * pairs + 12 * pairs,
         size=4 * PAIR * width,
-        scratch=[pltpu.VMEM((cells, 2 * PAIR), bf16)] * (blocks - 1),
+        scratch=[pltpu.VMEM((2 * PAIR, cells), bf16)] * (blocks - 1),
     )(consts, turn_weights, x_own, *others)
 
     def couplings():
@@ -357,7 +362,7 @@
     def sine_parts(halves):
         return call(
             functools.partial(sine_kernel, len(halves)),
-            [shape((cells, width), bf16)] * len(halves),
+            [shape((width, cells), bf16)] * len(halves),
             "sines",
             flops=12 * pairs,
             transcendentals=pairs,

time: 29.9 us -> 29.3 us (0.980)
  Pallas kernels: 13.9 us -> 12.7 us
  waiting for transfers between devices: 4.22 us -> 4.75 us
    pallas_call x7, Pallas kernels: 13.9 us -> 12.7 us  [run(): pl.pallas_call(kernel, out_shape=out_shape, in_specs=in_specs or [VMEM_SP...]
    ppermute x3, waiting for transfers between devices: 0.01 us -> 0.56 us  [rotated(): lax.ppermute(x, 'cell', [((i + shift) % count, i) for i in range(count)])]
  transfers between devices with their start and end apart: 9 -> 9, of which waited for: 3 -> 4; matrix products, arithmetic and copies ran while one was open for 0% -> 0% of each run, Pallas kernels for 42% -> 41%
where the time goes in v3:
time: 29.3 us; the launch traced here: 29.1 us
  Pallas kernels  12.7 us (43%)
  starting transfers between devices  9.57 us (33%)
  waiting for transfers between devices  4.75 us (16%)
  between operations  1.39 us (5%)
  other arithmetic  0.69 us (2%)
    pallas_call x7, Pallas kernels, run(): pl.pallas_call(kernel, out_shape=out_shape, in_specs=in_specs or [VMEM_SP...  12.7 us
    ppermute x6, starting transfers between devices, swapped(): lax.ppermute(x, 'study', [(i, partner(i, k)) for i in range(count)])  8.99 us
    ppermute x6, waiting for transfers between devices, swapped(): lax.ppermute(x, 'study', [(i, partner(i, k)) for i in range(count)])  4.19 us
    broadcast_in_dim x1, other arithmetic, on_device(): return jnp.swapaxes(own_part + out, 0, 1)[None]  0.67 us
  transfers between devices with their start and end apart: 9, of which 4 were waited for; matrix products, arithmetic and copies ran while one was open for 0% of the time, Pallas kernels for 41%

profile of v3, /device:TPU:0, one launch (start us, length us, event | category | flops | bytes accessed | tf_op | source)
XLA Modules:
  0.0 29.1 jit_solution(4489947717861634042)
XLA Ops:
  0.0 0.5 %collective-permute-start = (bf16[64,512]{1,0:T(8,128)(2,1)}, bf16[64,512]{1,0:T(8,128)(2,1)S(1)}, u32[]{:S(2)}, u32[]{:S(2)}) collective-permute-start(bf16[64,512]{1,0:T(8,128)(2,1)} %bitcast.8), channel_id=1, source_target_pairs={{1,0},{0,1},{3,2},{2,3},{5,4},{4,5},{7,6},{6,7},{9,8},{8,9},{11,10... | collective-permute-start | bytes 196616 | tf_op jit(solution)/shard_map/ppermute | solution.py:280
  0.5 0.1 collective-permute-start.4
  1.8 1.5 %setup.1 = (bf16[256,4096]{1,0:T(8,128)(2,1)S(1)}, bf16[64,4096]{1,0:T(8,128)(2,1)S(1)}, bf16[64,512]{1,0:T(8,128)(2,1)S(1)}, bf16[256,512]{1,0:T(8,128)(2,1)S(1)}, f32[1,128]{1,0:T(1,128)S(1)}) custom-call(s32[1]{0:T(128)S(6)} %copy.7.length_ref, bf16[64,8192]{1,0:T(8,128)(2,1)} %freq_hbm.1, f32[1,8192]{1,0:T(1,128)} %bitcast.10, bf16[64,512]{1,0:T(8,128)(2,1)} %bitcast.9), custom_call_target="tpu_custom_call" | custom-call | flops 5242880 | bytes 1048576 | tf_op jit(solution)/shard_map/setup/pallas_call | solution.py:258
  3.4 0.0 collective-permute-done.refs_0_.refs_1_
  3.4 6.4 %cosine_sums.1 = (f32[4096,512]{1,0:T(8,128)S(1)}, f32[4096,512]{1,0:T(8,128)S(1)}, f32[8,512]{1,0:T(8,128)S(1)}) custom-call(f32[1,128]{1,0:T(1,128)S(1)} %get-tuple-element.29.const_ref, bf16[256,4096]{1,0:T(8,128)(2,1)S(1)} %get-tuple-element.30.w_ref, bf16[256,512]{1,0:T(8,128)(2,1)S(1)} %get-tuple-element.31.x_own_ref, ...), custom_call_target="tpu_custom_call" | custom-call | flops 2197815296 | bytes 2097152 | tf_op jit(solution)/shard_map/cosine_sums/pallas_call | solution.py:258
  9.8 4.0 %collective-permute-start.1 = (f32[8,512]{1,0:T(8,128)S(1)}, f32[8,512]{1,0:T(8,128)S(1)}, u32[]{:S(2)}, u32[]{:S(2)}) collective-permute-start(f32[8,512]{1,0:T(8,128)S(1)} %get-tuple-element.33.mean_ref), channel_id=1, source_target_pairs={{0,6},{2,4},{4,2},{6,0},{8,14},{10,12},{12,10},{14,8},{16,22},{18,... | collective-permute-start | bytes 49160 | tf_op jit(solution)/shard_map/ppermute | solution.py:301
  13.8 0.5 %collective-permute-start.2 = (f32[8,512]{1,0:T(8,128)S(1)}, f32[8,512]{1,0:T(8,128)S(1)}, u32[]{:S(2)}, u32[]{:S(2)}) collective-permute-start(f32[8,512]{1,0:T(8,128)S(1)} %get-tuple-element.33.mean_ref), channel_id=1, source_target_pairs={{0,4},{2,6},{4,0},{6,2},{8,12},{10,14},{12,8},{14,10},{16,20},{18,... | collective-permute-start | bytes 49160 | tf_op jit(solution)/shard_map/ppermute | solution.py:301
  14.3 0.1 collective-permute-start.3
  14.4 1.5 %sines.2.s_ref = bf16[4096,512]{1,0:T(8,128)(2,1)S(1)} custom-call(f32[4096,512]{1,0:T(8,128)S(1)} %get-tuple-element.38.refs_0_), custom_call_target="tpu_custom_call" | custom-call | flops 50331648 | bytes 25165824 | tf_op jit(solution)/shard_map/sines/pallas_call | solution.py:258
  15.9 0.2 coupling.1
  16.2 1.3 %collective-permute-done.2 = f32[8,512]{1,0:T(8,128)S(1)} collective-permute-done((f32[8,512]{1,0:T(8,128)S(1)}, f32[8,512]{1,0:T(8,128)S(1)}, u32[]{:S(2)}, u32[]{:S(2)}) %collective-permute-start.2) | collective-permute-done | bytes 16416 | tf_op jit(solution)/shard_map/ppermute | solution.py:301
  17.5 0.5 %collective-permute-done.3 = f32[8,512]{1,0:T(8,128)S(1)} collective-permute-done((f32[8,512]{1,0:T(8,128)S(1)}, f32[8,512]{1,0:T(8,128)S(1)}, u32[]{:S(2)}, u32[]{:S(2)}) %collective-permute-start.3) | collective-permute-done | bytes 16416 | tf_op jit(solution)/shard_map/ppermute | solution.py:301
  18.0 3.6 %collective-permute-start.5 = (f32[8,512]{1,0:T(8,128)S(1)}, f32[8,512]{1,0:T(8,128)S(1)}, u32[]{:S(2)}, u32[]{:S(2)}) collective-permute-start(f32[8,512]{1,0:T(8,128)S(1)} %add_add_fusion.1), channel_id=1, source_target_pairs={{0,24},{2,26},{4,28},{6,30},{8,16},{10,18},{12,20},{14,22},{16,8},... | collective-permute-start | bytes 49160 | tf_op jit(solution)/shard_map/ppermute | solution.py:301
  21.6 0.0 collective-permute-start.6
  21.6 0.8 %collective-permute-start.7 = (f32[8,512]{1,0:T(8,128)S(1)}, f32[8,512]{1,0:T(8,128)S(1)}, u32[]{:S(2)}, u32[]{:S(2)}) collective-permute-start(f32[8,512]{1,0:T(8,128)S(1)} %add_add_fusion.1), channel_id=1, source_target_pairs={{0,8},{2,10},{4,12},{6,14},{8,0},{10,2},{12,4},{14,6},{16,24},{18,... | collective-permute-start | bytes 49160 | tf_op jit(solution)/shard_map/ppermute | solution.py:301
  22.4 1.5 %sines.3.s_ref = bf16[4096,512]{1,0:T(8,128)(2,1)S(1)} custom-call(f32[4096,512]{1,0:T(8,128)S(1)} %get-tuple-element.43.refs_0_), custom_call_target="tpu_custom_call" | custom-call | flops 50331648 | bytes 25165824 | tf_op jit(solution)/shard_map/sines/pallas_call | solution.py:258
  23.9 0.0 collective-permute-done.5
  23.9 2.3 %collective-permute-done.6 = f32[8,512]{1,0:T(8,128)S(1)} collective-permute-done((f32[8,512]{1,0:T(8,128)S(1)}, f32[8,512]{1,0:T(8,128)S(1)}, u32[]{:S(2)}, u32[]{:S(2)}) %collective-permute-start.6) | collective-permute-done | bytes 16416 | tf_op jit(solution)/shard_map/ppermute | solution.py:301
  26.2 0.0 collective-permute-done.7
  26.3 0.7 %residual_part.1 = (f32[64,512]{1,0:T(8,128)S(1)}, bf16[128,4096]{1,0:T(8,128)(2,1)S(1)}) custom-call(f32[1,128]{1,0:T(1,128)S(1)} %get-tuple-element.29.const_ref, f32[8,512]{1,0:T(8,128)S(1)} %add_add_fusion.sum_ref, f32[8,512]{1,0:T(8,128)S(1)} %get-tuple-element.33.mean_ref, bf16[64,4096]{1,0:T(8,128)(2,1)S(1)} %get-tuple-element.47.freq_ref, ...), custom_call_target="tpu_custom_call" | custom-call | flops 268435456 | bytes 4194304 | tf_op jit(solution)/shard_map/residual_part/pallas_call | solution.py:258
  27.0 0.1 collective-permute-start.8
  27.1 0.8 %own_part.1 = f32[64,512]{1,0:T(8,128)S(1)} custom-call(f32[1,128]{1,0:T(1,128)S(1)} %get-tuple-element.29.const_ref, bf16[4096,512]{1,0:T(8,128)(2,1)S(1)} %sines.3.s_ref, bf16[128,4096]{1,0:T(8,128)(2,1)S(1)} %get-tuple-element.50.rf_ref, f32[64,512]{1,0:T(8,128)S(1)} %get-tuple-element.51.refs_0_), custom_call_target="tpu_custom_call" | custom-call | flops 268435456 | bytes 4194304 | tf_op jit(solution)/shard_map/own_part/pallas_call | solution.py:258
  27.8 0.6 %collective-permute-done.8 = f32[64,512]{1,0:T(8,128)S(1)} collective-permute-done((f32[64,512]{1,0:T(8,128)S(1)}, f32[64,512]{1,0:T(8,128)S(1)}, u32[]{:S(2)}, u32[]{:S(2)}) %collective-permute-start.8) | collective-permute-done | bytes 131104 | tf_op jit(solution)/shard_map/ppermute | solution.py:280
  28.4 0.7 %add_bitcast_fusion = f32[1,512,64]{1,2,0:T(8,128)} fusion(f32[64,512]{1,0:T(8,128)S(1)} %own_part.1, f32[64,512]{1,0:T(8,128)S(1)} %collective-permute-done.8), kind=kLoop, calls=%fused_computation | loop fusion | flops 32768 | bytes 393216 | tf_op jit(solution)/shard_map/broadcast_in_dim | solution.py:407
  (6 shorter events, 0.0 us)
Async XLA Ops:
  0.0 3.4 %collective-permute-start = (bf16[64,512]{1,0:T(8,128)(2,1)}, bf16[64,512]{1,0:T(8,128)(2,1)S(1)}, u32[]{:S(2)}, u32[]{:S(2)}) collective-permute-start(bf16[64,512]{1,0:T(8,128)(2,1)} %bitcast.8), channel_id=1, source_target_pairs={{1,0},{0,1},{3,2},{2,3},{5,4},{4,5},{7,6},{6,7},{9,8},{8,9},{11,10... | collective-permute-start | bytes 196616 | tf_op jit(solution)/shard_map/ppermute | solution.py:280
  0.5 15.5 %collective-permute-start.4 = (s32[1,512]{1,0:T(1,128)}, s32[1,512]{1,0:T(1,128)S(1)}, u32[]{:S(2)}, u32[]{:S(2)}) collective-permute-start(s32[1,512]{1,0:T(1,128)} %refs_2_.1), channel_id=1, source_target_pairs={{1,0},{0,1},{3,2},{2,3},{5,4},{4,5},{7,6},{6,7},{9,8},{8,9},{11,10... | collective-permute-start | bytes 6152 | tf_op jit(solution)/shard_map/ppermute | solution.py:280
  9.8 6.3 %collective-permute-start.1 = (f32[8,512]{1,0:T(8,128)S(1)}, f32[8,512]{1,0:T(8,128)S(1)}, u32[]{:S(2)}, u32[]{:S(2)}) collective-permute-start(f32[8,512]{1,0:T(8,128)S(1)} %get-tuple-element.33.mean_ref), channel_id=1, source_target_pairs={{0,6},{2,4},{4,2},{6,0},{8,14},{10,12},{12,10},{14,8},{16,22},{18,... | collective-permute-start | bytes 49160 | tf_op jit(solution)/shard_map/ppermute | solution.py:301
  13.8 3.7 %collective-permute-start.2 = (f32[8,512]{1,0:T(8,128)S(1)}, f32[8,512]{1,0:T(8,128)S(1)}, u32[]{:S(2)}, u32[]{:S(2)}) collective-permute-start(f32[8,512]{1,0:T(8,128)S(1)} %get-tuple-element.33.mean_ref), channel_id=1, source_target_pairs={{0,4},{2,6},{4,0},{6,2},{8,12},{10,14},{12,8},{14,10},{16,20},{18,... | collective-permute-start | bytes 49160 | tf_op jit(solution)/shard_map/ppermute | solution.py:301
  14.3 3.7 %collective-permute-start.3 = (f32[8,512]{1,0:T(8,128)S(1)}, f32[8,512]{1,0:T(8,128)S(1)}, u32[]{:S(2)}, u32[]{:S(2)}) collective-permute-start(f32[8,512]{1,0:T(8,128)S(1)} %get-tuple-element.33.mean_ref), channel_id=1, source_target_pairs={{0,2},{2,0},{4,6},{6,4},{8,10},{10,8},{12,14},{14,12},{16,18},{18,... | collective-permute-start | bytes 49160 | tf_op jit(solution)/shard_map/ppermute | solution.py:301
  14.4 1.5 %copy-start = (s32[1,512]{1,0:T(1,128)S(1)}, s32[1,512]{1,0:T(1,128)}, u32[]{:S(2)}) copy-start(s32[1,512]{1,0:T(1,128)} %refs_2_.1) | copy-start | bytes 6148
  18.0 5.9 %collective-permute-start.5 = (f32[8,512]{1,0:T(8,128)S(1)}, f32[8,512]{1,0:T(8,128)S(1)}, u32[]{:S(2)}, u32[]{:S(2)}) collective-permute-start(f32[8,512]{1,0:T(8,128)S(1)} %add_add_fusion.1), channel_id=1, source_target_pairs={{0,24},{2,26},{4,28},{6,30},{8,16},{10,18},{12,20},{14,22},{16,8},... | collective-permute-start | bytes 49160 | tf_op jit(solution)/shard_map/ppermute | solution.py:301
  21.6 4.6 %collective-permute-start.6 = (f32[8,512]{1,0:T(8,128)S(1)}, f32[8,512]{1,0:T(8,128)S(1)}, u32[]{:S(2)}, u32[]{:S(2)}) collective-permute-start(f32[8,512]{1,0:T(8,128)S(1)} %add_add_fusion.1), channel_id=1, source_target_pairs={{0,16},{2,18},{4,20},{6,22},{8,24},{10,26},{12,28},{14,30},{16,0},... | collective-permute-start | bytes 49160 | tf_op jit(solution)/shard_map/ppermute | solution.py:301
  21.6 4.6 %collective-permute-start.7 = (f32[8,512]{1,0:T(8,128)S(1)}, f32[8,512]{1,0:T(8,128)S(1)}, u32[]{:S(2)}, u32[]{:S(2)}) collective-permute-start(f32[8,512]{1,0:T(8,128)S(1)} %add_add_fusion.1), channel_id=1, source_target_pairs={{0,8},{2,10},{4,12},{6,14},{8,0},{10,2},{12,4},{14,6},{16,24},{18,... | collective-permute-start | bytes 49160 | tf_op jit(solution)/shard_map/ppermute | solution.py:301
  27.0 1.4 %collective-permute-start.8 = (f32[64,512]{1,0:T(8,128)S(1)}, f32[64,512]{1,0:T(8,128)S(1)}, u32[]{:S(2)}, u32[]{:S(2)}) collective-permute-start(f32[64,512]{1,0:T(8,128)S(1)} %get-tuple-element.52), channel_id=1, source_target_pairs={{1,0},{0,1},{3,2},{2,3},{5,4},{4,5},{7,6},{6,7},{9,8},{8,9},{11,10... | collective-permute-start | bytes 393224 | tf_op jit(solution)/shard_map/ppermute | solution.py:280

commit v4 on v3

--- a/solution.py
+++ b/solution.py
@@ -280,13 +280,13 @@
     return lax.ppermute(x, "cell", [((i + shift) % count, i) for i in range(count)])
 
 
-def digits(count):
-    radices = []
-    while count > 1:
-        radix = next(r for r in (4, 2, *range(3, count + 1)) if count % r == 0)
-        radices.append(radix)
-        count //= radix
-    return radices
+def rounds(count):
+    stride = 1
+    while stride < count:
+        left = count // stride
+        radix = 4 if stride == 1 and left % 4 == 0 else next(r for r in range(2, left + 1) if left % r == 0)
+        yield stride, radix
+        stride *= radix
 
 
 def swapped(x, stride, radix):
@@ -370,18 +370,20 @@
         )(*halves)
 
     study_penalty_weight, mean = lax.optimization_barrier((study_penalty_weight, mean))
-    center, stride, beside = mean, 1, []
-    for turn, radix in enumerate(digits(studies)):
+    center, own_half, done = mean, halves[0], []
+    steps = [lambda: sine_parts(halves[1:]), couplings, lambda: sine_parts([own_half])]
+    for stride, radix in rounds(studies):
         parts = swapped(center, stride, radix)
-        stride *= radix
-        if turn == 0:
-            bases, sines = couplings(), sine_parts(halves[1:])
-            beside = [*bases, *sines, *halves[:1]]
-        elif turn == 1:
-            sines = [*sine_parts(beside[-1:]), *beside[len(bases) : -1]]
-            beside = [*beside[: len(bases)], *sines]
-        center, *beside = lax.optimization_barrier((sum(parts, center), *beside))
-    bases, sines = beside[: len(bases)], beside[len(bases) :]
+        made = steps[len(done)]() if len(done) < len(steps) else []
+        later = [own_half] if len(done) < len(steps) - 1 else []
+        center, *made = lax.optimization_barrier((sum(parts, center), *made, *later))
+        if later:
+            own_half = made.pop()
+        if len(done) < len(steps):
+            done.append(made)
+    while len(done) < len(steps):
+        done.append(steps[len(done)]())
+    sines, bases = [*done[2], *done[0]], done[1]
 
     out, residual_freq = None, None
     part_shape = shape((depth, cells), f32)

time: 29.3 us -> 28.2 us (0.962)
  starting transfers between devices: 9.57 us -> 8.84 us
    ppermute x6 -> x5, starting transfers between devices: 8.99 us -> 8.31 us  [swapped(): lax.ppermute(x, 'study', [(i, partner(i, k)) for i in range(count)])]
    ppermute x6 -> x5, waiting for transfers between devices: 4.19 us -> 3.93 us  [swapped(): lax.ppermute(x, 'study', [(i, partner(i, k)) for i in range(count)])]
  transfers between devices with their start and end apart: 9 -> 8, of which waited for: 4 -> 5; matrix products, arithmetic and copies ran while one was open for 0% -> 0% of each run, Pallas kernels for 41% -> 20%
where the time goes in v4:
time: 28.2 us; the launch traced here: 28.1 us
  Pallas kernels  12.7 us (45%)
  starting transfers between devices  8.84 us (31%)
  waiting for transfers between devices  4.48 us (16%)
  between operations  1.39 us (5%)
  other arithmetic  0.69 us (2%)
    pallas_call x7, Pallas kernels, run(): pl.pallas_call(kernel, out_shape=out_shape, in_specs=in_specs or [VMEM_SP...  12.7 us
    ppermute x5, starting transfers between devices, swapped(): lax.ppermute(x, 'study', [(i, partner(i, k)) for i in range(count)])  8.31 us
    ppermute x5, waiting for transfers between devices, swapped(): lax.ppermute(x, 'study', [(i, partner(i, k)) for i in range(count)])  3.93 us
    broadcast_in_dim x1, other arithmetic, on_device(): return jnp.swapaxes(own_part + out, 0, 1)[None]  0.67 us
  transfers between devices with their start and end apart: 8, of which 5 were waited for; matrix products, arithmetic and copies ran while one was open for 0% of the time, Pallas kernels for 20%

profile of v4, /device:TPU:0, one launch (start us, length us, event | category | flops | bytes accessed | tf_op | source)
XLA Modules:
  0.0 28.1 jit_solution(6011257767833666239)
XLA Ops:
  0.0 0.5 %collective-permute-start = (bf16[64,512]{1,0:T(8,128)(2,1)}, bf16[64,512]{1,0:T(8,128)(2,1)S(1)}, u32[]{:S(2)}, u32[]{:S(2)}) collective-permute-start(bf16[64,512]{1,0:T(8,128)(2,1)} %bitcast.8), channel_id=1, source_target_pairs={{1,0},{0,1},{3,2},{2,3},{5,4},{4,5},{7,6},{6,7},{9,8},{8,9},{11,10... | collective-permute-start | bytes 196616 | tf_op jit(solution)/shard_map/ppermute | solution.py:280
  1.1 1.5 %setup.1 = (bf16[256,4096]{1,0:T(8,128)(2,1)S(1)}, bf16[64,4096]{1,0:T(8,128)(2,1)S(1)}, bf16[64,512]{1,0:T(8,128)(2,1)S(1)}, bf16[256,512]{1,0:T(8,128)(2,1)S(1)}, f32[1,128]{1,0:T(1,128)S(1)}) custom-call(s32[1]{0:T(128)S(6)} %copy.7.length_ref, bf16[64,8192]{1,0:T(8,128)(2,1)} %freq_hbm.1, f32[1,8192]{1,0:T(1,128)} %bitcast.10, bf16[64,512]{1,0:T(8,128)(2,1)} %bitcast.9), custom_call_target="tpu_custom_call" | custom-call | flops 5242880 | bytes 1048576 | tf_op jit(solution)/shard_map/setup/pallas_call | solution.py:258
  2.6 0.0 copy-start
  2.7 0.0 collective-permute-done.refs_0_.refs_1_
  2.7 6.4 %cosine_sums.1 = (f32[4096,512]{1,0:T(8,128)S(1)}, f32[4096,512]{1,0:T(8,128)S(1)}, f32[8,512]{1,0:T(8,128)S(1)}) custom-call(f32[1,128]{1,0:T(1,128)S(1)} %get-tuple-element.28.const_ref, bf16[256,4096]{1,0:T(8,128)(2,1)S(1)} %get-tuple-element.29.w_ref, bf16[256,512]{1,0:T(8,128)(2,1)S(1)} %get-tuple-element.30.x_own_ref, ...), custom_call_target="tpu_custom_call" | custom-call | flops 2197815296 | bytes 2097152 | tf_op jit(solution)/shard_map/cosine_sums/pallas_call | solution.py:258
  9.1 3.5 %collective-permute-start.1 = (f32[8,512]{1,0:T(8,128)S(1)}, f32[8,512]{1,0:T(8,128)S(1)}, u32[]{:S(2)}, u32[]{:S(2)}) collective-permute-start(f32[8,512]{1,0:T(8,128)S(1)} %get-tuple-element.32.mean_ref), channel_id=1, source_target_pairs={{0,6},{2,4},{4,2},{6,0},{8,14},{10,12},{12,10},{14,8},{16,22},{18,... | collective-permute-start | bytes 49160 | tf_op jit(solution)/shard_map/ppermute | solution.py:301
  12.6 0.5 %collective-permute-start.2 = (f32[8,512]{1,0:T(8,128)S(1)}, f32[8,512]{1,0:T(8,128)S(1)}, u32[]{:S(2)}, u32[]{:S(2)}) collective-permute-start(f32[8,512]{1,0:T(8,128)S(1)} %get-tuple-element.32.mean_ref), channel_id=1, source_target_pairs={{0,4},{2,6},{4,0},{6,2},{8,12},{10,14},{12,8},{14,10},{16,20},{18,... | collective-permute-start | bytes 49160 | tf_op jit(solution)/shard_map/ppermute | solution.py:301
  13.1 0.1 collective-permute-start.3
  13.3 0.0 collective-permute-start.5
  13.9 1.5 %sines.2.s_ref = bf16[4096,512]{1,0:T(8,128)(2,1)S(1)} custom-call(f32[4096,512]{1,0:T(8,128)S(1)} %get-tuple-element.33.refs_0_), custom_call_target="tpu_custom_call" | custom-call | flops 50331648 | bytes 25165824 | tf_op jit(solution)/shard_map/sines/pallas_call | solution.py:258
  15.4 0.0 collective-permute-done.1
  15.4 0.9 %collective-permute-done.2 = f32[8,512]{1,0:T(8,128)S(1)} collective-permute-done((f32[8,512]{1,0:T(8,128)S(1)}, f32[8,512]{1,0:T(8,128)S(1)}, u32[]{:S(2)}, u32[]{:S(2)}) %collective-permute-start.2) | collective-permute-done | bytes 16416 | tf_op jit(solution)/shard_map/ppermute | solution.py:301
  16.4 0.5 %collective-permute-done.3 = f32[8,512]{1,0:T(8,128)S(1)} collective-permute-done((f32[8,512]{1,0:T(8,128)S(1)}, f32[8,512]{1,0:T(8,128)S(1)}, u32[]{:S(2)}, u32[]{:S(2)}) %collective-permute-start.3) | collective-permute-done | bytes 16416 | tf_op jit(solution)/shard_map/ppermute | solution.py:301
  16.9 1.6 %collective-permute-start.4 = (f32[8,512]{1,0:T(8,128)S(1)}, f32[8,512]{1,0:T(8,128)S(1)}, u32[]{:S(2)}, u32[]{:S(2)}) collective-permute-start(f32[8,512]{1,0:T(8,128)S(1)} %add_add_fusion), channel_id=1, source_target_pairs={{0,8},{2,10},{4,12},{6,14},{8,0},{10,2},{12,4},{14,6},{16,24},{18,... | collective-permute-start | bytes 49160 | tf_op jit(solution)/shard_map/ppermute | solution.py:301
  18.4 0.2 coupling.1
  18.7 2.0 %collective-permute-done.4 = f32[8,512]{1,0:T(8,128)S(1)} collective-permute-done((f32[8,512]{1,0:T(8,128)S(1)}, f32[8,512]{1,0:T(8,128)S(1)}, u32[]{:S(2)}, u32[]{:S(2)}) %collective-permute-start.4) | collective-permute-done | bytes 16416 | tf_op jit(solution)/shard_map/ppermute | solution.py:301
  20.6 2.6 %collective-permute-start.6 = (f32[8,512]{1,0:T(8,128)S(1)}, f32[8,512]{1,0:T(8,128)S(1)}, u32[]{:S(2)}, u32[]{:S(2)}) collective-permute-start(f32[8,512]{1,0:T(8,128)S(1)} %add.21), channel_id=1, source_target_pairs={{0,16},{2,18},{4,20},{6,22},{8,24},{10,26},{12,28},{14,30},{16,0},... | collective-permute-start | bytes 49160 | tf_op jit(solution)/shard_map/ppermute | solution.py:301
  23.2 1.5 %sines.3.s_ref = bf16[4096,512]{1,0:T(8,128)(2,1)S(1)} custom-call(f32[4096,512]{1,0:T(8,128)S(1)} %get-tuple-element.42.refs_0_), custom_call_target="tpu_custom_call" | custom-call | flops 50331648 | bytes 25165824 | tf_op jit(solution)/shard_map/sines/pallas_call | solution.py:258
  24.7 0.5 %collective-permute-done.6 = f32[8,512]{1,0:T(8,128)S(1)} collective-permute-done((f32[8,512]{1,0:T(8,128)S(1)}, f32[8,512]{1,0:T(8,128)S(1)}, u32[]{:S(2)}, u32[]{:S(2)}) %collective-permute-start.6) | collective-permute-done | bytes 16416 | tf_op jit(solution)/shard_map/ppermute | solution.py:301
  25.3 0.7 %residual_part.1 = (f32[64,512]{1,0:T(8,128)S(1)}, bf16[128,4096]{1,0:T(8,128)(2,1)S(1)}) custom-call(f32[1,128]{1,0:T(1,128)S(1)} %get-tuple-element.28.const_ref, f32[8,512]{1,0:T(8,128)S(1)} %add.22.sum_ref, f32[8,512]{1,0:T(8,128)S(1)} %get-tuple-element.32.mean_ref, bf16[64,4096]{1,0:T(8,128)(2,1)S(1)} %get-tuple-element.45.freq_ref, ...), custom_call_target="tpu_custom_call" | custom-call | flops 268435456 | bytes 4194304 | tf_op jit(solution)/shard_map/residual_part/pallas_call | solution.py:258
  26.0 0.1 collective-permute-start.7
  26.1 0.8 %own_part.1 = f32[64,512]{1,0:T(8,128)S(1)} custom-call(f32[1,128]{1,0:T(1,128)S(1)} %get-tuple-element.28.const_ref, bf16[4096,512]{1,0:T(8,128)(2,1)S(1)} %sines.3.s_ref, bf16[128,4096]{1,0:T(8,128)(2,1)S(1)} %get-tuple-element.48.rf_ref, f32[64,512]{1,0:T(8,128)S(1)} %get-tuple-element.49.refs_0_), custom_call_target="tpu_custom_call" | custom-call | flops 268435456 | bytes 4194304 | tf_op jit(solution)/shard_map/own_part/pallas_call | solution.py:258
  26.8 0.5 %collective-permute-done.7 = f32[64,512]{1,0:T(8,128)S(1)} collective-permute-done((f32[64,512]{1,0:T(8,128)S(1)}, f32[64,512]{1,0:T(8,128)S(1)}, u32[]{:S(2)}, u32[]{:S(2)}) %collective-permute-start.7) | collective-permute-done | bytes 131104 | tf_op jit(solution)/shard_map/ppermute | solution.py:280
  27.4 0.7 %add_bitcast_fusion = f32[1,512,64]{1,2,0:T(8,128)} fusion(f32[64,512]{1,0:T(8,128)S(1)} %own_part.1, f32[64,512]{1,0:T(8,128)S(1)} %collective-permute-done.7), kind=kLoop, calls=%fused_computation | loop fusion | flops 32768 | bytes 393216 | tf_op jit(solution)/shard_map/broadcast_in_dim | solution.py:409
  (5 shorter events, 0.0 us)
Async XLA Ops:
  0.0 2.7 %collective-permute-start = (bf16[64,512]{1,0:T(8,128)(2,1)}, bf16[64,512]{1,0:T(8,128)(2,1)S(1)}, u32[]{:S(2)}, u32[]{:S(2)}) collective-permute-start(bf16[64,512]{1,0:T(8,128)(2,1)} %bitcast.8), channel_id=1, source_target_pairs={{1,0},{0,1},{3,2},{2,3},{5,4},{4,5},{7,6},{6,7},{9,8},{8,9},{11,10... | collective-permute-start | bytes 196616 | tf_op jit(solution)/shard_map/ppermute | solution.py:280
  2.6 10.6 %copy-start = (s32[1,512]{1,0:T(1,128)S(1)}, s32[1,512]{1,0:T(1,128)}, u32[]{:S(2)}) copy-start(s32[1,512]{1,0:T(1,128)} %refs_2_.1) | copy-start | bytes 6148
  9.1 6.3 %collective-permute-start.1 = (f32[8,512]{1,0:T(8,128)S(1)}, f32[8,512]{1,0:T(8,128)S(1)}, u32[]{:S(2)}, u32[]{:S(2)}) collective-permute-start(f32[8,512]{1,0:T(8,128)S(1)} %get-tuple-element.32.mean_ref), channel_id=1, source_target_pairs={{0,6},{2,4},{4,2},{6,0},{8,14},{10,12},{12,10},{14,8},{16,22},{18,... | collective-permute-start | bytes 49160 | tf_op jit(solution)/shard_map/ppermute | solution.py:301
  12.6 3.7 %collective-permute-start.2 = (f32[8,512]{1,0:T(8,128)S(1)}, f32[8,512]{1,0:T(8,128)S(1)}, u32[]{:S(2)}, u32[]{:S(2)}) collective-permute-start(f32[8,512]{1,0:T(8,128)S(1)} %get-tuple-element.32.mean_ref), channel_id=1, source_target_pairs={{0,4},{2,6},{4,0},{6,2},{8,12},{10,14},{12,8},{14,10},{16,20},{18,... | collective-permute-start | bytes 49160 | tf_op jit(solution)/shard_map/ppermute | solution.py:301
  13.1 3.7 %collective-permute-start.3 = (f32[8,512]{1,0:T(8,128)S(1)}, f32[8,512]{1,0:T(8,128)S(1)}, u32[]{:S(2)}, u32[]{:S(2)}) collective-permute-start(f32[8,512]{1,0:T(8,128)S(1)} %get-tuple-element.32.mean_ref), channel_id=1, source_target_pairs={{0,2},{2,0},{4,6},{6,4},{8,10},{10,8},{12,14},{14,12},{16,18},{18,... | collective-permute-start | bytes 49160 | tf_op jit(solution)/shard_map/ppermute | solution.py:301
  13.3 5.2 %collective-permute-start.5 = (s32[1,512]{1,0:T(1,128)S(1)}, s32[1,512]{1,0:T(1,128)S(1)}, u32[]{:S(2)}, u32[]{:S(2)}) collective-permute-start(s32[1,512]{1,0:T(1,128)S(1)} %copy-done), channel_id=1, source_target_pairs={{1,0},{0,1},{3,2},{2,3},{5,4},{4,5},{7,6},{6,7},{9,8},{8,9},{11,10... | collective-permute-start | bytes 6152 | tf_op jit(solution)/shard_map/ppermute | solution.py:280
  16.9 3.7 %collective-permute-start.4 = (f32[8,512]{1,0:T(8,128)S(1)}, f32[8,512]{1,0:T(8,128)S(1)}, u32[]{:S(2)}, u32[]{:S(2)}) collective-permute-start(f32[8,512]{1,0:T(8,128)S(1)} %add_add_fusion), channel_id=1, source_target_pairs={{0,8},{2,10},{4,12},{6,14},{8,0},{10,2},{12,4},{14,6},{16,24},{18,... | collective-permute-start | bytes 49160 | tf_op jit(solution)/shard_map/ppermute | solution.py:301
  20.6 4.6 %collective-permute-start.6 = (f32[8,512]{1,0:T(8,128)S(1)}, f32[8,512]{1,0:T(8,128)S(1)}, u32[]{:S(2)}, u32[]{:S(2)}) collective-permute-start(f32[8,512]{1,0:T(8,128)S(1)} %add.21), channel_id=1, source_target_pairs={{0,16},{2,18},{4,20},{6,22},{8,24},{10,26},{12,28},{14,30},{16,0},... | collective-permute-start | bytes 49160 | tf_op jit(solution)/shard_map/ppermute | solution.py:301
  26.0 1.4 %collective-permute-start.7 = (f32[64,512]{1,0:T(8,128)S(1)}, f32[64,512]{1,0:T(8,128)S(1)}, u32[]{:S(2)}, u32[]{:S(2)}) collective-permute-start(f32[64,512]{1,0:T(8,128)S(1)} %get-tuple-element.50), channel_id=1, source_target_pairs={{1,0},{0,1},{3,2},{2,3},{5,4},{4,5},{7,6},{6,7},{9,8},{8,9},{11,10... | collective-permute-start | bytes 393224 | tf_op jit(solution)/shard_map/ppermute | solution.py:280

commit v5 on v4

v5 whole, which is shorter than its diff:
```python
import functools
import math
from typing import NamedTuple

import jax
import jax.numpy as jnp
from jax import lax
from jax.experimental import pallas as pl
from jax.experimental.pallas import tpu as pltpu
from jax.sharding import PartitionSpec as P

DONOR_LABELS = 16
FEATURE_PENALTY = 16.0
BLOCK = 1024
PAIR = 128
WIDE_CORE = 1
SHIFT = 4
LANES = 128
PHASE_ROWS = 16
SUBLANES = 8
MIB = 1 << 20

COS_LEAD = -0.552051508388134
COS_TERMS = (-4.602194203577409, 9.359560663732573, -5.6907268683441155)
SIN_LEAD = 2.0 * COS_LEAD * abs(COS_LEAD)

VMEM_SPEC = pl.BlockSpec(memory_space=pltpu.VMEM)
SMEM_SPEC = pl.BlockSpec(memory_space=pltpu.SMEM)
HBM_SPEC = pl.BlockSpec(memory_space=pltpu.HBM)


def split3(x):
    hi = x.astype(jnp.bfloat16)
    rest = x - hi.astype(jnp.float32)
    mid = rest.astype(jnp.bfloat16)
    low = (rest - mid.astype(jnp.float32)).astype(jnp.bfloat16)
    return hi, mid, low


def block_start(block, cells):
    count = lax.axis_size("cell")
    return lax.rem(lax.axis_index("cell") + block, count) * cells


def valid_row(block, cells, length):
    position = lax.broadcasted_iota(jnp.int32, (1, cells), 1) + block_start(block, cells)
    return (position.astype(jnp.float32) < length).astype(jnp.float32)


class Split(NamedTuple):
    features: int
    narrow: int
    wide: int

    @property
    def scale(self):
        return math.sqrt(2.0 / self.features)

    @property
    def rows(self):
        return next(r for r in range(SUBLANES, 0, -1) if self.wide % (r * LANES) == 0)

    def start(self):
        return pl.multiple_of(lax.axis_index("cell") * self.narrow, LANES)

    def extra(self, body):
        if self.wide > self.narrow:
            pl.when(lax.axis_index("cell") == WIDE_CORE)(body)

    def over_blocks(self, body):
        def over(start, stop):
            for offset in range(start, stop, BLOCK):
                body(offset, min(BLOCK, stop - offset))

        over(0, self.narrow)
        self.extra(lambda: over(self.narrow, self.wide))


def split_features(features, blocks):
    even = features // blocks
    shift = even * SHIFT // (LANES * 32) * LANES if blocks == 2 else 0
    return Split(features, even - shift, even + shift)


def store_cells(x_ref, z, valid):
    depth, cells = z.shape
    z = (z.astype(jnp.float32) * valid).astype(jnp.bfloat16)
    for part in range(3):
        x_ref[part * depth : (part + 1) * depth, :] = z
    tail = x_ref.shape[0] - 3 * depth
    ones = jnp.where(lax.broadcasted_iota(jnp.int32, (tail, cells), 0) < 3, valid, 0.0)
    x_ref[3 * depth :, :] = ones.astype(jnp.bfloat16)


def setup_kernel(split, length_ref, freq_hbm, phase_hbm, z_hbm, w_ref, freq_ref, z_ref, x_ref, const_ref, phase_buf, sems):
    depth, width = freq_ref.shape
    start = split.start()
    copies = [
        pltpu.make_async_copy(source, target, sems.at[i])
        for i, (source, target) in enumerate(
            [
                (z_hbm, z_ref),
                (phase_hbm.at[:, pl.ds(start, width)], phase_buf),
                (freq_hbm.at[:, pl.ds(start, width)], freq_ref),
            ]
        )
    ]
    for copy in copies:
        copy.start()
    length = jnp.full((1, 1), length_ref[0], jnp.int32).astype(jnp.float32)
    const_ref[...] = jnp.broadcast_to(length, const_ref.shape)
    row = 3 * depth + PHASE_ROWS
    w_ref[row:, :] = jnp.zeros((2 * PAIR - row, width), jnp.bfloat16)
    copies[0].wait()
    store_cells(x_ref, z_ref[...], valid_row(0, z_ref.shape[1], length))
    for copy in copies[1:]:
        copy.wait()
    turn = 1.0 / (2.0 * math.pi)
    for part, rows in enumerate(split3(freq_ref[...].astype(jnp.float32) * turn)):
        w_ref[part * depth : (part + 1) * depth, :] = rows
    hi, mid, low = [p.astype(jnp.float32) for p in split3(phase_buf[...] * turn)]
    index = lax.broadcasted_iota(jnp.int32, (PHASE_ROWS, width), 0)
    rows = jnp.where(index == 0, hi, jnp.where(index == 1, mid, jnp.where(index == 2, low, 0.0)))
    w_ref[3 * depth : row, :] = rows.astype(jnp.bfloat16)


def cosine_kernel(split, blocks, const_ref, w_ref, x_own_ref, *refs):
    z_refs = refs[: blocks - 1]
    s_refs = refs[blocks - 1 : 2 * blocks - 1]
    mean_ref = refs[2 * blocks - 1]
    x_refs = [x_own_ref, *refs[2 * blocks :]]
    width, cells = s_refs[0].shape
    length = const_ref[0:1, 0:1]
    for block in range(1, blocks):
        store_cells(x_refs[block], z_refs[block - 1][...], valid_row(block, cells, length))
    scale = split.scale
    per_length = 1.0 / length
    a, b, c = COS_TERMS
    strip = mean_ref.shape[1]
    mean_ref[...] = jnp.zeros_like(mean_ref)

    def one_block(offset, size):
        here = slice(offset, offset + size)
        weights = w_ref[:, here].T
        squares = jnp.zeros((size, LANES), jnp.float32)
        for x_ref, s_ref in zip(x_refs, s_refs):
            t = jnp.dot(weights, x_ref[...], preferred_element_type=jnp.float32)
            r = t - jnp.round(t)
            u = r * r
            s = r * (((u + a) * u + b) * u + c)
            s_ref[here, :] = s
            for lane in range(0, cells, LANES):
                part = s[:, lane : lane + LANES]
                squares += part * part
        squares = jnp.sum(squares.T, axis=0, keepdims=True)
        mean = scale - (2.0 * scale * COS_LEAD * COS_LEAD) * per_length * squares
        for piece in range(0, size, LANES):
            row, column = divmod(offset + piece, strip)
            mean_ref[row : row + 1, column : column + LANES] = mean[:, piece : piece + LANES]

    split.over_blocks(one_block)


def sine_kernel(split, blocks, *refs):
    top = (1.0 + 2e-6) / (COS_LEAD * COS_LEAD)

    def one_block(offset, size):
        here = slice(offset, offset + size)
        for s_ref, out_ref in zip(refs[:blocks], refs[blocks:]):
            s = s_ref[here, :]
            rest = top - s * s
            out_ref[here, :] = (s * (rest * lax.rsqrt(rest))).astype(jnp.bfloat16)

    split.over_blocks(one_block)


def stacked(rows, cells):
    index = lax.broadcasted_iota(jnp.int32, (DONOR_LABELS, cells), 0)
    total = jnp.zeros((DONOR_LABELS, cells), jnp.float32)
    for k, row in enumerate(rows):
        if row is not None:
            total = jnp.where(index == k, row, total)
    return total.astype(jnp.bfloat16)


def coupling_kernel(blocks, weight_ref, const_ref, *refs):
    z_refs, donor_refs, out_refs = refs[:blocks], refs[blocks : 2 * blocks], refs[2 * blocks :]
    depth, cells = out_refs[0].shape
    window = blocks * cells
    f32, bf16 = jnp.float32, jnp.bfloat16
    length = const_ref[0:1, 0:1]
    inverse_n = 1.0 / length
    label = lax.broadcasted_iota(jnp.int32, (DONOR_LABELS, cells), 0)
    members = [(ref[...] == label).astype(f32) for ref in donor_refs]
    valids = [valid_row(block, cells, length) for block in range(blocks)]
    counts = sum(
        jnp.sum(member * valid, axis=1, keepdims=True)
        for member, valid in zip(members, valids)
    )
    inverse = 1.0 / jnp.maximum(counts, 1.0)
    present = jnp.sum((counts > 0.5).astype(f32), axis=0, keepdims=True)
    one = jnp.ones((1, 1), f32)
    wides = [ref[...].astype(f32) for ref in z_refs]
    norms = [
        [p.astype(f32) for p in split3(-0.5 * jnp.sum(z * z, axis=0, keepdims=True))]
        for z in wides
    ]
    shares = [
        inverse_n * jnp.sum(member * inverse, axis=0, keepdims=True) for member in members
    ]
    same_zero = jnp.zeros((3 * DONOR_LABELS, cells), bf16)
    z_zero = jnp.zeros((depth, cells), bf16)
    rights = []
    for target in range(len(out_refs)):
        rest = [p.astype(f32) for p in split3(present * inverse_n * inverse_n - shares[target])]
        member = members[target].astype(bf16)
        exponent = [z_refs[target][...], stacked([one] * 3 + norms[target], cells), same_zero]
        pair = [z_zero, stacked([None] * 6 + [one] * 3 + rest, cells), member, member, member]
        rights.append(
            jnp.concatenate(
                [jnp.concatenate(exponent, axis=0), jnp.concatenate(pair, axis=0)], axis=1
            )
        )
    totals = [jnp.zeros((PAIR, cells), f32) for _ in out_refs]
    for source in range(blocks):
        valid = valids[source]
        z = z_refs[source][...]
        minus = [p.astype(f32) for p in split3(-shares[source] * valid)]
        left = jnp.concatenate(
            [
                z,
                stacked(norms[source] + [one] * 3 + minus + [valid] * 3, cells),
                *split3(members[source] * (inverse * inverse) * valid),
            ],
            axis=0,
        ).astype(f32).T.astype(bf16)
        rows = jnp.concatenate([z, jnp.ones((PAIR - depth, cells), bf16)], axis=0)
        for target, right in enumerate(rights):
            both = jnp.dot(left, right, preferred_element_type=f32)
            coupling = both[:, cells:] * jnp.exp2(both[:, :cells] * (math.log2(math.e) / depth))
            hi = coupling.astype(bf16)
            low = (coupling - hi.astype(f32)).astype(bf16)
            totals[target] += jnp.dot(rows, hi, preferred_element_type=f32)
            totals[target] += jnp.dot(rows, low, preferred_element_type=f32)
    scale = -(2.0 * window / depth) * jnp.full((1, 1), weight_ref[0], f32)
    for target, out_ref in enumerate(out_refs):
        total = totals[target]
        gradient = wides[target] * total[depth : depth + 1] - total[:depth]
        out_ref[...] = scale * valids[target] * gradient


def residual_kernel(split, block, window, const_ref, sum_ref, mean_ref, freq_ref, s_ref, *refs):
    *base_refs, out_ref, rf_ref = refs
    rows, strip = sum_ref.shape
    depth = freq_ref.shape[0]
    center = sum_ref[...] * (1.0 / lax.axis_size("study"))
    residual = (2.0 * FEATURE_PENALTY) * (mean_ref[...] - center)
    for row in range(rows):
        here = slice(row * strip, (row + 1) * strip)
        product = freq_ref[:, here].astype(jnp.float32) * residual[row : row + 1]
        hi = product.astype(jnp.bfloat16)
        rf_ref[:depth, here] = hi
        rf_ref[depth:, here] = (product - hi.astype(jnp.float32)).astype(jnp.bfloat16)
    part_kernel(split, block, window, const_ref, s_ref, rf_ref, *base_refs, out_ref)


def part_kernel(split, block, window, const_ref, s_ref, rf_ref, *refs):
    *base_refs, out_ref = refs
    depth, cells = out_ref.shape
    length = const_ref[0:1, 0:1]
    factor = -(SIN_LEAD * window * split.scale) / length * valid_row(block, cells, length)

    def part(here):
        both = jnp.dot(rf_ref[:, here], s_ref[here, :], preferred_element_type=jnp.float32)
        return factor * (both[:depth] + both[depth:])

    out_ref[...] = sum((ref[...] for ref in base_refs), part(slice(0, split.narrow)))

    def add_extra():
        out_ref[...] += part(slice(split.narrow, split.wide))

    split.extra(add_extra)


def call(kernel, out_shape, name, flops, transcendentals=0, size=0, scratch=(), vmem=8, in_specs=None):
    several = isinstance(out_shape, (list, tuple))

    def run(*operands):
        return pl.pallas_call(
            kernel,
            out_shape=out_shape,
            in_specs=in_specs or [VMEM_SPEC] * len(operands),
            out_specs=[VMEM_SPEC] * len(out_shape) if several else VMEM_SPEC,
            scratch_shapes=list(scratch),
            compiler_params=pltpu.CompilerParams(vmem_limit_bytes=vmem * MIB),
            cost_estimate=pl.CostEstimate(
                flops=int(flops), bytes_accessed=int(size), transcendentals=int(transcendentals)
            ),
            name=name,
        )(*operands)

    return run


def in_hbm(x):
    return pltpu.with_memory_space_constraint(x, pltpu.HBM)


def rotated(x, shift):
    count = lax.axis_size("cell")
    return lax.ppermute(x, "cell", [((i + shift) % count, i) for i in range(count)])


def rounds(count):
    stride = 1
    while stride < count:
        left = count // stride
        radix = 4 if stride == 1 and left % 4 == 0 else next(r for r in range(2, left + 1) if left % r == 0)
        yield stride, radix
        stride *= radix


def swapped(x, stride, radix):
    count = lax.axis_size("study")

    def partner(i, k):
        digit = i // stride % radix
        other = digit ^ k if radix & (radix - 1) == 0 else (digit + k) % radix
        return i + (other - digit) * stride

    return [
        lax.ppermute(x, "study", [(i, partner(i, k)) for i in range(count)])
        for k in range(1, radix)
    ]


def on_device(latents, donor_ids, study_valid_length, study_penalty_weight, frequencies, phases):
    own = jnp.swapaxes(latents[0], 0, 1)
    depth, cells = own.shape
    blocks = lax.axis_size("cell")
    studies = lax.axis_size("study")
    features = frequencies.shape[1]
    split = split_features(features, blocks)
    width = split.wide
    window = blocks * cells
    mean_shape = (split.rows, width // split.rows)
    f32, bf16 = jnp.float32, jnp.bfloat16
    shape = jax.ShapeDtypeStruct
    pairs = window * width

    others = [rotated(own, k) for k in range(1, blocks)]
    donors = [donor_ids] + [rotated(donor_ids, k) for k in range(1, blocks)]

    turn_weights, freq_part, own, x_own, consts = call(
        functools.partial(setup_kernel, split),
        [
            shape((2 * PAIR, width), bf16),
            shape((depth, width), bf16),
            shape((depth, cells), bf16),
            shape((2 * PAIR, cells), bf16),
            shape((1, 128), f32),
        ],
        "setup",
        flops=20 * depth * width,
        size=4 * depth * width,
        scratch=[pltpu.VMEM((1, width), f32), pltpu.SemaphoreType.DMA((3,))],
        in_specs=[SMEM_SPEC] + [HBM_SPEC] * 3,
    )(
        study_valid_length,
        *[in_hbm(x) for x in (frequencies, phases.reshape(1, features), own)],
    )

    *halves, mean = call(
        functools.partial(cosine_kernel, split, blocks),
        [shape((width, cells), f32)] * blocks + [shape(mean_shape, f32)],
        "cosine_sums",
        flops=4 * PAIR * pairs + 12 * pairs,
        size=4 * PAIR * width,
        scratch=[pltpu.VMEM((2 * PAIR, cells), bf16)] * (blocks - 1),
    )(consts, turn_weights, x_own, *others)

    def couplings():
        return call(
            functools.partial(coupling_kernel, blocks),
            [shape((depth, cells), f32)],
            "coupling",
            flops=2 * cells * window * (3 * depth),
            transcendentals=cells * window,
            size=4 * cells * depth,
            in_specs=[SMEM_SPEC] + [VMEM_SPEC] * (1 + 2 * blocks),
        )(study_penalty_weight, consts, own, *others, *donors)

    def sine_parts(halves):
        return call(
            functools.partial(sine_kernel, split, len(halves)),
            [shape((width, cells), bf16)] * len(halves),
            "sines",
            flops=12 * pairs,
            transcendentals=pairs,
            size=6 * pairs,
        )(*halves)

    study_penalty_weight, mean = lax.optimization_barrier((study_penalty_weight, mean))
    center, own_half, done = mean, halves[0], []
    steps = [lambda: sine_parts(halves[1:]), couplings, lambda: sine_parts([own_half])]
    for stride, radix in rounds(studies):
        parts = swapped(center, stride, radix)
        made = steps[len(done)]() if len(done) < len(steps) else []
        later = [own_half] if len(done) < len(steps) - 1 else []
        center, *made = lax.optimization_barrier((sum(parts, center), *made, *later))
        if later:
            own_half = made.pop()
        if len(done) < len(steps):
            done.append(made)
    while len(done) < len(steps):
        done.append(steps[len(done)]())
    sines, bases = [*done[2], *done[0]], done[1]

    out, residual_freq = None, None
    part_shape = shape((depth, cells), f32)
    cost = dict(flops=2 * cells * width * depth, size=2 * cells * width)
    for block in range(1, blocks):
        base = bases[block : block + 1]
        if residual_freq is None:
            part, residual_freq = call(
                functools.partial(residual_kernel, split, block, window),
                [part_shape, shape((2 * depth, width), bf16)],
                "residual_part",
                **cost,
            )(consts, center, mean, freq_part, sines[block], *base)
        else:
            part = call(
                functools.partial(part_kernel, split, block, window), part_shape, "other_part", **cost
            )(consts, sines[block], residual_freq, *base)
        sent = rotated(part, blocks - block)
        out = sent if out is None else out + sent
    own_part = call(functools.partial(part_kernel, split, 0, window), part_shape, "own_part", **cost)(
        consts, sines[0], residual_freq, bases[0]
    )
    return jnp.swapaxes(own_part + out, 0, 1)[None]


def solution(mesh):
    in_specs = (P("study", "cell", None), P("study", "cell"), P("study"), P("study"), P(), P())
    out_specs = P("study", "cell", None)
    return jax.shard_map(
        on_device, mesh=mesh, in_specs=in_specs, out_specs=out_specs, check_vma=False
    )
```

time: 28.2 us -> 28.1 us (level)
  waiting for transfers between devices: 4.48 us -> 2.07 us
  starting transfers between devices: 8.84 us -> 10.9 us
    ppermute x5, waiting for transfers between devices: 3.93 us -> 1.38 us  [swapped(): lax.ppermute(x, 'study', [(i, partner(i, k)) for i in range(count)])]
    ppermute x3, starting transfers between devices: 0.53 us -> 2.26 us  [rotated(): lax.ppermute(x, 'cell', [((i + shift) % count, i) for i in range(count)])]
    ppermute x5, starting transfers between devices: 8.31 us -> 8.64 us  [swapped(): lax.ppermute(x, 'study', [(i, partner(i, k)) for i in range(count)])]
  transfers between devices with their start and end apart: 8 -> 8, of which waited for: 5 -> 3; matrix products, arithmetic and copies ran while one was open for 0% -> 0% of each run, Pallas kernels for 20% -> 23%
where the time goes in v5:
time: 28.1 us; the launch traced here: 27.9 us
  Pallas kernels  12.8 us (46%)
  starting transfers between devices  10.9 us (39%)
  waiting for transfers between devices  2.07 us (7%)
  between operations  1.41 us (5%)
  other arithmetic  0.7 us (2%)
    pallas_call x7, Pallas kernels, run(): pl.pallas_call(kernel, out_shape=out_shape, in_specs=in_specs or [VMEM_SP...  12.8 us
    ppermute x5, starting transfers between devices, swapped(): lax.ppermute(x, 'study', [(i, partner(i, k)) for i in range(count)])  8.64 us
    ppermute x3, starting transfers between devices, rotated(): lax.ppermute(x, 'cell', [((i + shift) % count, i) for i in range(count)])  2.26 us
    ppermute x5, waiting for transfers between devices, swapped(): lax.ppermute(x, 'study', [(i, partner(i, k)) for i in range(count)])  1.38 us
    ppermute x3, waiting for transfers between devices, rotated(): lax.ppermute(x, 'cell', [((i + shift) % count, i) for i in range(count)])  0.68 us
    broadcast_in_dim x1, other arithmetic, on_device(): return jnp.swapaxes(own_part + out, 0, 1)[None]  0.68 us
  transfers between devices with their start and end apart: 8, of which 3 were waited for; matrix products, arithmetic and copies ran while one was open for 0% of the time, Pallas kernels for 23%

profile of v5, /device:TPU:0, one launch (start us, length us, event | category | flops | bytes accessed | tf_op | source)
XLA Modules:
  0.0 27.9 jit_solution(2749778745502751275)
XLA Ops:
  0.0 0.5 %collective-permute-start = (bf16[64,512]{1,0:T(8,128)(2,1)}, bf16[64,512]{1,0:T(8,128)(2,1)S(1)}, u32[]{:S(2)}, u32[]{:S(2)}) collective-permute-start(bf16[64,512]{1,0:T(8,128)(2,1)} %bitcast.8), channel_id=1, source_target_pairs={{1,0},{0,1},{3,2},{2,3},{5,4},{4,5},{7,6},{6,7},{9,8},{8,9},{11,10... | collective-permute-start | bytes 196616 | tf_op jit(solution)/shard_map/ppermute | solution.py:311
  1.1 1.6 %setup.1 = (bf16[256,4608]{1,0:T(8,128)(2,1)S(1)}, bf16[64,4608]{1,0:T(8,128)(2,1)S(1)}, bf16[64,512]{1,0:T(8,128)(2,1)S(1)}, bf16[256,512]{1,0:T(8,128)(2,1)S(1)}, f32[1,128]{1,0:T(1,128)S(1)}) custom-call(s32[1]{0:T(128)S(6)} %copy.7.length_ref, bf16[64,8192]{1,0:T(8,128)(2,1)} %freq_hbm.1, f32[1,8192]{1,0:T(1,128)} %bitcast.10, bf16[64,512]{1,0:T(8,128)(2,1)} %bitcast.9), custom_call_target="tpu_custom_call" | custom-call | flops 5898240 | bytes 1179648 | tf_op jit(solution)/shard_map/setup/pallas_call | solution.py:289
  2.7 0.0 copy-start
  2.7 0.0 collective-permute-done.refs_0_.refs_1_
  2.7 5.7 %cosine_sums.1 = (f32[4608,512]{1,0:T(8,128)S(1)}, f32[4608,512]{1,0:T(8,128)S(1)}, f32[6,768]{1,0:T(8,128)S(1)}) custom-call(f32[1,128]{1,0:T(1,128)S(1)} %get-tuple-element.25.const_ref, bf16[256,4608]{1,0:T(8,128)(2,1)S(1)} %get-tuple-element.26.w_ref, bf16[256,512]{1,0:T(8,128)(2,1)S(1)} %get-tuple-element.27.x_own_ref, ...), custom_call_target="tpu_custom_call" | custom-call | flops 2472542208 | bytes 2359296 | tf_op jit(solution)/shard_map/cosine_sums/pallas_call | solution.py:289
  8.4 3.5 %collective-permute-start.3 = (f32[6,768]{1,0:T(8,128)S(1)}, f32[6,768]{1,0:T(8,128)S(1)}, u32[]{:S(2)}, u32[]{:S(2)}) collective-permute-start(f32[6,768]{1,0:T(8,128)S(1)} %get-tuple-element.29.mean_ref), channel_id=1, source_target_pairs={{0,6},{2,4},{4,2},{6,0},{8,14},{10,12},{12,10},{14,8},{16,22},{18,... | collective-permute-start | bytes 55304 | tf_op jit(solution)/shard_map/ppermute | solution.py:332
  11.9 0.5 %collective-permute-start.2 = (f32[6,768]{1,0:T(8,128)S(1)}, f32[6,768]{1,0:T(8,128)S(1)}, u32[]{:S(2)}, u32[]{:S(2)}) collective-permute-start(f32[6,768]{1,0:T(8,128)S(1)} %get-tuple-element.29.mean_ref), channel_id=1, source_target_pairs={{0,4},{2,6},{4,0},{6,2},{8,12},{10,14},{12,8},{14,10},{16,20},{18,... | collective-permute-start | bytes 55304 | tf_op jit(solution)/shard_map/ppermute | solution.py:332
  12.4 0.1 collective-permute-start.1
  12.6 1.7 %collective-permute-start.5 = (s32[1,512]{1,0:T(1,128)S(1)}, s32[1,512]{1,0:T(1,128)S(1)}, u32[]{:S(2)}, u32[]{:S(2)}) collective-permute-start(s32[1,512]{1,0:T(1,128)S(1)} %copy-done), channel_id=1, source_target_pairs={{1,0},{0,1},{3,2},{2,3},{5,4},{4,5},{7,6},{6,7},{9,8},{8,9},{11,10... | collective-permute-start | bytes 6152 | tf_op jit(solution)/shard_map/ppermute | solution.py:311
  14.9 1.5 %sines.2.s_ref = bf16[4608,512]{1,0:T(8,128)(2,1)S(1)} custom-call(f32[4608,512]{1,0:T(8,128)S(1)} %get-tuple-element.30.refs_0_), custom_call_target="tpu_custom_call" | custom-call | flops 56623104 | bytes 28311552 | tf_op jit(solution)/shard_map/sines/pallas_call | solution.py:289
  16.5 0.0 collective-permute-done.2
  16.5 0.0 collective-permute-done.1
  16.5 1.8 %collective-permute-start.4 = (f32[6,768]{1,0:T(8,128)S(1)}, f32[6,768]{1,0:T(8,128)S(1)}, u32[]{:S(2)}, u32[]{:S(2)}) collective-permute-start(f32[6,768]{1,0:T(8,128)S(1)} %add_add_fusion), channel_id=1, source_target_pairs={{0,8},{2,10},{4,12},{6,14},{8,0},{10,2},{12,4},{14,6},{16,24},{18,... | collective-permute-start | bytes 55304 | tf_op jit(solution)/shard_map/ppermute | solution.py:332
  18.3 0.0 collective-permute-done.5.refs_3_
  18.3 1.5 %coupling.1.refs_0_ = f32[64,512]{1,0:T(8,128)S(1)} custom-call(f32[1]{0:T(128)S(6)} %copy.8.weight_ref, f32[1,128]{1,0:T(1,128)S(1)} %get-tuple-element.25.const_ref, bf16[64,512]{1,0:T(8,128)(2,1)S(1)} %get-tuple-element.34.refs_0_, bf16[64,512]{1,0:T(8,128)(2,1)S(1)} %collective-permute-done.refs_0_.refs_1_, s32[1,512]{1,0:T(1,128)S(1)} %copy-done, ...), custom_call_target="tpu_custom_call" | custom-call | flops 201326592 | bytes 131072 | tf_op jit(solution)/shard_map/coupling/pallas_call | solution.py:289
  19.7 0.7 %collective-permute-done.4 = f32[6,768]{1,0:T(8,128)S(1)} collective-permute-done((f32[6,768]{1,0:T(8,128)S(1)}, f32[6,768]{1,0:T(8,128)S(1)}, u32[]{:S(2)}, u32[]{:S(2)}) %collective-permute-start.4) | collective-permute-done | bytes 18464 | tf_op jit(solution)/shard_map/ppermute | solution.py:332
  20.4 2.7 %collective-permute-start.6 = (f32[6,768]{1,0:T(8,128)S(1)}, f32[6,768]{1,0:T(8,128)S(1)}, u32[]{:S(2)}, u32[]{:S(2)}) collective-permute-start(f32[6,768]{1,0:T(8,128)S(1)} %add.21), channel_id=1, source_target_pairs={{0,16},{2,18},{4,20},{6,22},{8,24},{10,26},{12,28},{14,30},{16,0},... | collective-permute-start | bytes 55304 | tf_op jit(solution)/shard_map/ppermute | solution.py:332
  23.1 1.3 %sines.3.s_ref = bf16[4608,512]{1,0:T(8,128)(2,1)S(1)} custom-call(f32[4608,512]{1,0:T(8,128)S(1)} %get-tuple-element.37.refs_0_), custom_call_target="tpu_custom_call" | custom-call | flops 56623104 | bytes 28311552 | tf_op jit(solution)/shard_map/sines/pallas_call | solution.py:289
  24.4 0.7 %collective-permute-done.6 = f32[6,768]{1,0:T(8,128)S(1)} collective-permute-done((f32[6,768]{1,0:T(8,128)S(1)}, f32[6,768]{1,0:T(8,128)S(1)}, u32[]{:S(2)}, u32[]{:S(2)}) %collective-permute-start.6) | collective-permute-done | bytes 18464 | tf_op jit(solution)/shard_map/ppermute | solution.py:332
  25.1 0.7 %residual_part.1 = (f32[64,512]{1,0:T(8,128)S(1)}, bf16[128,4608]{1,0:T(8,128)(2,1)S(1)}) custom-call(f32[1,128]{1,0:T(1,128)S(1)} %get-tuple-element.25.const_ref, f32[6,768]{1,0:T(8,128)S(1)} %add.22.sum_ref, f32[6,768]{1,0:T(8,128)S(1)} %get-tuple-element.29.mean_ref, bf16[64,4608]{1,0:T(8,128)(2,1)S(1)} %get-tuple-element.40.freq_ref, ...), custom_call_target="tpu_custom_call" | custom-call | flops 301989888 | bytes 4718592 | tf_op jit(solution)/shard_map/residual_part/pallas_call | solution.py:289
  25.8 0.1 collective-permute-start.7
  25.9 0.6 %own_part.1 = f32[64,512]{1,0:T(8,128)S(1)} custom-call(f32[1,128]{1,0:T(1,128)S(1)} %get-tuple-element.25.const_ref, bf16[4608,512]{1,0:T(8,128)(2,1)S(1)} %sines.3.s_ref, bf16[128,4608]{1,0:T(8,128)(2,1)S(1)} %get-tuple-element.42.rf_ref, f32[64,512]{1,0:T(8,128)S(1)} %coupling.1.refs_0_), custom_call_target="tpu_custom_call" | custom-call | flops 301989888 | bytes 4718592 | tf_op jit(solution)/shard_map/own_part/pallas_call | solution.py:289
  26.5 0.7 %collective-permute-done.7 = f32[64,512]{1,0:T(8,128)S(1)} collective-permute-done((f32[64,512]{1,0:T(8,128)S(1)}, f32[64,512]{1,0:T(8,128)S(1)}, u32[]{:S(2)}, u32[]{:S(2)}) %collective-permute-start.7) | collective-permute-done | bytes 131104 | tf_op jit(solution)/shard_map/ppermute | solution.py:311
  27.2 0.7 %add_bitcast_fusion = f32[1,512,64]{1,2,0:T(8,128)} fusion(f32[64,512]{1,0:T(8,128)S(1)} %own_part.1, f32[64,512]{1,0:T(8,128)S(1)} %collective-permute-done.7), kind=kLoop, calls=%fused_computation | loop fusion | flops 32768 | bytes 393216 | tf_op jit(solution)/shard_map/broadcast_in_dim | solution.py:440
  (5 shorter events, 0.0 us)
Async XLA Ops:
  0.0 2.7 %collective-permute-start = (bf16[64,512]{1,0:T(8,128)(2,1)}, bf16[64,512]{1,0:T(8,128)(2,1)S(1)}, u32[]{:S(2)}, u32[]{:S(2)}) collective-permute-start(bf16[64,512]{1,0:T(8,128)(2,1)} %bitcast.8), channel_id=1, source_target_pairs={{1,0},{0,1},{3,2},{2,3},{5,4},{4,5},{7,6},{6,7},{9,8},{8,9},{11,10... | collective-permute-start | bytes 196616 | tf_op jit(solution)/shard_map/ppermute | solution.py:311
  2.7 9.8 %copy-start = (s32[1,512]{1,0:T(1,128)S(1)}, s32[1,512]{1,0:T(1,128)}, u32[]{:S(2)}) copy-start(s32[1,512]{1,0:T(1,128)} %refs_2_.1) | copy-start | bytes 6148
  8.4 8.0 %collective-permute-start.3 = (f32[6,768]{1,0:T(8,128)S(1)}, f32[6,768]{1,0:T(8,128)S(1)}, u32[]{:S(2)}, u32[]{:S(2)}) collective-permute-start(f32[6,768]{1,0:T(8,128)S(1)} %get-tuple-element.29.mean_ref), channel_id=1, source_target_pairs={{0,6},{2,4},{4,2},{6,0},{8,14},{10,12},{12,10},{14,8},{16,22},{18,... | collective-permute-start | bytes 55304 | tf_op jit(solution)/shard_map/ppermute | solution.py:332
  11.9 4.5 %collective-permute-start.2 = (f32[6,768]{1,0:T(8,128)S(1)}, f32[6,768]{1,0:T(8,128)S(1)}, u32[]{:S(2)}, u32[]{:S(2)}) collective-permute-start(f32[6,768]{1,0:T(8,128)S(1)} %get-tuple-element.29.mean_ref), channel_id=1, source_target_pairs={{0,4},{2,6},{4,0},{6,2},{8,12},{10,14},{12,8},{14,10},{16,20},{18,... | collective-permute-start | bytes 55304 | tf_op jit(solution)/shard_map/ppermute | solution.py:332
  12.4 4.1 %collective-permute-start.1 = (f32[6,768]{1,0:T(8,128)S(1)}, f32[6,768]{1,0:T(8,128)S(1)}, u32[]{:S(2)}, u32[]{:S(2)}) collective-permute-start(f32[6,768]{1,0:T(8,128)S(1)} %get-tuple-element.29.mean_ref), channel_id=1, source_target_pairs={{0,2},{2,0},{4,6},{6,4},{8,10},{10,8},{12,14},{14,12},{16,18},{18,... | collective-permute-start | bytes 55304 | tf_op jit(solution)/shard_map/ppermute | solution.py:332
  12.6 5.7 %collective-permute-start.5 = (s32[1,512]{1,0:T(1,128)S(1)}, s32[1,512]{1,0:T(1,128)S(1)}, u32[]{:S(2)}, u32[]{:S(2)}) collective-permute-start(s32[1,512]{1,0:T(1,128)S(1)} %copy-done), channel_id=1, source_target_pairs={{1,0},{0,1},{3,2},{2,3},{5,4},{4,5},{7,6},{6,7},{9,8},{8,9},{11,10... | collective-permute-start | bytes 6152 | tf_op jit(solution)/shard_map/ppermute | solution.py:311
  16.5 3.9 %collective-permute-start.4 = (f32[6,768]{1,0:T(8,128)S(1)}, f32[6,768]{1,0:T(8,128)S(1)}, u32[]{:S(2)}, u32[]{:S(2)}) collective-permute-start(f32[6,768]{1,0:T(8,128)S(1)} %add_add_fusion), channel_id=1, source_target_pairs={{0,8},{2,10},{4,12},{6,14},{8,0},{10,2},{12,4},{14,6},{16,24},{18,... | collective-permute-start | bytes 55304 | tf_op jit(solution)/shard_map/ppermute | solution.py:332
  20.4 4.7 %collective-permute-start.6 = (f32[6,768]{1,0:T(8,128)S(1)}, f32[6,768]{1,0:T(8,128)S(1)}, u32[]{:S(2)}, u32[]{:S(2)}) collective-permute-start(f32[6,768]{1,0:T(8,128)S(1)} %add.21), channel_id=1, source_target_pairs={{0,16},{2,18},{4,20},{6,22},{8,24},{10,26},{12,28},{14,30},{16,0},... | collective-permute-start | bytes 55304 | tf_op jit(solution)/shard_map/ppermute | solution.py:332
  25.8 1.4 %collective-permute-start.7 = (f32[64,512]{1,0:T(8,128)S(1)}, f32[64,512]{1,0:T(8,128)S(1)}, u32[]{:S(2)}, u32[]{:S(2)}) collective-permute-start(f32[64,512]{1,0:T(8,128)S(1)} %get-tuple-element.44), channel_id=1, source_target_pairs={{1,0},{0,1},{3,2},{2,3},{5,4},{4,5},{7,6},{6,7},{9,8},{8,9},{11,10... | collective-permute-start | bytes 393224 | tf_op jit(solution)/shard_map/ppermute | solution.py:311

commit v6 on v5

--- a/solution.py
+++ b/solution.py
@@ -14,7 +14,7 @@
 BLOCK = 1024
 PAIR = 128
 WIDE_CORE = 1
-SHIFT = 4
+SHIFT = 6
 LANES = 128
 PHASE_ROWS = 16
 SUBLANES = 8

time: 28.1 us -> 27.9 us (level)
  starting transfers between devices: 10.9 us -> 12.2 us
  waiting for transfers between devices: 2.07 us -> 1.17 us
  Pallas kernels: 12.8 us -> 12.3 us
    ppermute x3, starting transfers between devices: 2.26 us -> 3.46 us  [rotated(): lax.ppermute(x, 'cell', [((i + shift) % count, i) for i in range(count)])]
    ppermute x5, waiting for transfers between devices: 1.38 us -> 0.8 us  [swapped(): lax.ppermute(x, 'study', [(i, partner(i, k)) for i in range(count)])]
    pallas_call x7, Pallas kernels: 12.8 us -> 12.3 us  [run(): pl.pallas_call(kernel, out_shape=out_shape, in_specs=in_specs or [VMEM_SP...]
    ppermute x3, waiting for transfers between devices: 0.68 us -> 0.37 us  [rotated(): lax.ppermute(x, 'cell', [((i + shift) % count, i) for i in range(count)])]
where the time goes in v6:
time: 27.9 us; the launch traced here: 27.8 us
  Pallas kernels  12.3 us (44%)
  starting transfers between devices  12.2 us (44%)
  between operations  1.42 us (5%)
  waiting for transfers between devices  1.17 us (4%)
  other arithmetic  0.72 us (3%)
    pallas_call x7, Pallas kernels, run(): pl.pallas_call(kernel, out_shape=out_shape, in_specs=in_specs or [VMEM_SP...  12.3 us
    ppermute x5, starting transfers between devices, swapped(): lax.ppermute(x, 'study', [(i, partner(i, k)) for i in range(count)])  8.72 us
    ppermute x3, starting transfers between devices, rotated(): lax.ppermute(x, 'cell', [((i + shift) % count, i) for i in range(count)])  3.46 us
    ppermute x5, waiting for transfers between devices, swapped(): lax.ppermute(x, 'study', [(i, partner(i, k)) for i in range(count)])  0.8 us
    broadcast_in_dim x1, other arithmetic, on_device(): return jnp.swapaxes(own_part + out, 0, 1)[None]  0.67 us
  transfers between devices with their start and end apart: 8, of which 3 were waited for; matrix products, arithmetic and copies ran while one was open for 0% of the time, Pallas kernels for 23%

profile of v6, /device:TPU:0, one launch (start us, length us, event | category | flops | bytes accessed | tf_op | source)
XLA Modules:
  0.0 27.8 jit_solution(3615367297386963159)
XLA Ops:
  0.0 0.5 %collective-permute-start = (bf16[64,512]{1,0:T(8,128)(2,1)}, bf16[64,512]{1,0:T(8,128)(2,1)S(1)}, u32[]{:S(2)}, u32[]{:S(2)}) collective-permute-start(bf16[64,512]{1,0:T(8,128)(2,1)} %bitcast.8), channel_id=1, source_target_pairs={{1,0},{0,1},{3,2},{2,3},{5,4},{4,5},{7,6},{6,7},{9,8},{8,9},{11,10... | collective-permute-start | bytes 196616 | tf_op jit(solution)/shard_map/ppermute | solution.py:311
  1.1 1.6 %setup.1 = (bf16[256,4864]{1,0:T(8,128)(2,1)S(1)}, bf16[64,4864]{1,0:T(8,128)(2,1)S(1)}, bf16[64,512]{1,0:T(8,128)(2,1)S(1)}, bf16[256,512]{1,0:T(8,128)(2,1)S(1)}, f32[1,128]{1,0:T(1,128)S(1)}) custom-call(s32[1]{0:T(128)S(6)} %copy.7.length_ref, bf16[64,8192]{1,0:T(8,128)(2,1)} %freq_hbm.1, f32[1,8192]{1,0:T(1,128)} %bitcast.10, bf16[64,512]{1,0:T(8,128)(2,1)} %bitcast.9), custom_call_target="tpu_custom_call" | custom-call | flops 6225920 | bytes 1245184 | tf_op jit(solution)/shard_map/setup/pallas_call | solution.py:289
  2.8 0.0 copy-start
  2.8 0.0 collective-permute-done.refs_0_.refs_1_
  2.8 5.3 %cosine_sums.1 = (f32[4864,512]{1,0:T(8,128)S(1)}, f32[4864,512]{1,0:T(8,128)S(1)}, f32[2,2432]{1,0:T(2,128)S(1)}) custom-call(f32[1,128]{1,0:T(1,128)S(1)} %get-tuple-element.25.const_ref, bf16[256,4864]{1,0:T(8,128)(2,1)S(1)} %get-tuple-element.26.w_ref, bf16[256,512]{1,0:T(8,128)(2,1)S(1)} %get-tuple-element.27.x_own_ref, ...), custom_call_target="tpu_custom_call" | custom-call | flops 2609905664 | bytes 2490368 | tf_op jit(solution)/shard_map/cosine_sums/pallas_call | solution.py:289
  8.1 3.5 %collective-permute-start.3 = (f32[2,2432]{1,0:T(2,128)S(1)}, f32[2,2432]{1,0:T(2,128)S(1)}, u32[]{:S(2)}, u32[]{:S(2)}) collective-permute-start(f32[2,2432]{1,0:T(2,128)S(1)} %get-tuple-element.29.mean_ref), channel_id=1, source_target_pairs={{0,6},{2,4},{4,2},{6,0},{8,14},{10,12},{12,10},{14,8},{16,22},{18,... | collective-permute-start | bytes 58376 | tf_op jit(solution)/shard_map/ppermute | solution.py:332
  11.6 0.5 %collective-permute-start.2 = (f32[2,2432]{1,0:T(2,128)S(1)}, f32[2,2432]{1,0:T(2,128)S(1)}, u32[]{:S(2)}, u32[]{:S(2)}) collective-permute-start(f32[2,2432]{1,0:T(2,128)S(1)} %get-tuple-element.29.mean_ref), channel_id=1, source_target_pairs={{0,4},{2,6},{4,0},{6,2},{8,12},{10,14},{12,8},{14,10},{16,20},{18,... | collective-permute-start | bytes 58376 | tf_op jit(solution)/shard_map/ppermute | solution.py:332
  12.1 0.1 collective-permute-start.1
  12.3 2.5 %collective-permute-start.5 = (s32[1,512]{1,0:T(1,128)S(1)}, s32[1,512]{1,0:T(1,128)S(1)}, u32[]{:S(2)}, u32[]{:S(2)}) collective-permute-start(s32[1,512]{1,0:T(1,128)S(1)} %copy-done), channel_id=1, source_target_pairs={{1,0},{0,1},{3,2},{2,3},{5,4},{4,5},{7,6},{6,7},{9,8},{8,9},{11,10... | collective-permute-start | bytes 6152 | tf_op jit(solution)/shard_map/ppermute | solution.py:311
  14.8 1.4 %sines.2.s_ref = bf16[4864,512]{1,0:T(8,128)(2,1)S(1)} custom-call(f32[4864,512]{1,0:T(8,128)S(1)} %get-tuple-element.30.refs_0_), custom_call_target="tpu_custom_call" | custom-call | flops 59768832 | bytes 29884416 | tf_op jit(solution)/shard_map/sines/pallas_call | solution.py:289
  16.2 0.0 collective-permute-done.2
  16.2 0.0 collective-permute-done.1
  16.3 1.8 %collective-permute-start.4 = (f32[2,2432]{1,0:T(2,128)S(1)}, f32[2,2432]{1,0:T(2,128)S(1)}, u32[]{:S(2)}, u32[]{:S(2)}) collective-permute-start(f32[2,2432]{1,0:T(2,128)S(1)} %add_add_fusion), channel_id=1, source_target_pairs={{0,8},{2,10},{4,12},{6,14},{8,0},{10,2},{12,4},{14,6},{16,24},{18,... | collective-permute-start | bytes 58376 | tf_op jit(solution)/shard_map/ppermute | solution.py:332
  18.7 0.0 collective-permute-done.5.refs_3_
  18.7 1.5 %coupling.1.refs_0_ = f32[64,512]{1,0:T(8,128)S(1)} custom-call(f32[1]{0:T(128)S(6)} %copy.8.weight_ref, f32[1,128]{1,0:T(1,128)S(1)} %get-tuple-element.25.const_ref, bf16[64,512]{1,0:T(8,128)(2,1)S(1)} %get-tuple-element.34.refs_0_, bf16[64,512]{1,0:T(8,128)(2,1)S(1)} %collective-permute-done.refs_0_.refs_1_, s32[1,512]{1,0:T(1,128)S(1)} %copy-done, ...), custom_call_target="tpu_custom_call" | custom-call | flops 201326592 | bytes 131072 | tf_op jit(solution)/shard_map/coupling/pallas_call | solution.py:289
  20.1 0.1 collective-permute-done.4
  20.2 2.8 %collective-permute-start.6 = (f32[2,2432]{1,0:T(2,128)S(1)}, f32[2,2432]{1,0:T(2,128)S(1)}, u32[]{:S(2)}, u32[]{:S(2)}) collective-permute-start(f32[2,2432]{1,0:T(2,128)S(1)} %add.21), channel_id=1, source_target_pairs={{0,16},{2,18},{4,20},{6,22},{8,24},{10,26},{12,28},{14,30},{16,0},... | collective-permute-start | bytes 58376 | tf_op jit(solution)/shard_map/ppermute | solution.py:332
  23.0 1.2 %sines.3.s_ref = bf16[4864,512]{1,0:T(8,128)(2,1)S(1)} custom-call(f32[4864,512]{1,0:T(8,128)S(1)} %get-tuple-element.37.refs_0_), custom_call_target="tpu_custom_call" | custom-call | flops 59768832 | bytes 29884416 | tf_op jit(solution)/shard_map/sines/pallas_call | solution.py:289
  24.3 0.7 %collective-permute-done.6 = f32[2,2432]{1,0:T(2,128)S(1)} collective-permute-done((f32[2,2432]{1,0:T(2,128)S(1)}, f32[2,2432]{1,0:T(2,128)S(1)}, u32[]{:S(2)}, u32[]{:S(2)}) %collective-permute-start.6) | collective-permute-done | bytes 19488 | tf_op jit(solution)/shard_map/ppermute | solution.py:332
  25.0 0.6 %residual_part.1 = (f32[64,512]{1,0:T(8,128)S(1)}, bf16[128,4864]{1,0:T(8,128)(2,1)S(1)}) custom-call(f32[1,128]{1,0:T(1,128)S(1)} %get-tuple-element.25.const_ref, f32[2,2432]{1,0:T(2,128)S(1)} %add.22.sum_ref, f32[2,2432]{1,0:T(2,128)S(1)} %get-tuple-element.29.mean_ref, bf16[64,4864]{1,0:T(8,128)(2,1)S(1)} %get-tuple-element.40.freq_ref, ...), custom_call_target="tpu_custom_call" | custom-call | flops 318767104 | bytes 4980736 | tf_op jit(solution)/shard_map/residual_part/pallas_call | solution.py:289
  25.6 0.5 %collective-permute-start.7 = (f32[64,512]{1,0:T(8,128)S(1)}, f32[64,512]{1,0:T(8,128)S(1)}, u32[]{:S(2)}, u32[]{:S(2)}) collective-permute-start(f32[64,512]{1,0:T(8,128)S(1)} %get-tuple-element.44), channel_id=1, source_target_pairs={{1,0},{0,1},{3,2},{2,3},{5,4},{4,5},{7,6},{6,7},{9,8},{8,9},{11,10... | collective-permute-start | bytes 393224 | tf_op jit(solution)/shard_map/ppermute | solution.py:311
  26.1 0.6 %own_part.1 = f32[64,512]{1,0:T(8,128)S(1)} custom-call(f32[1,128]{1,0:T(1,128)S(1)} %get-tuple-element.25.const_ref, bf16[4864,512]{1,0:T(8,128)(2,1)S(1)} %sines.3.s_ref, bf16[128,4864]{1,0:T(8,128)(2,1)S(1)} %get-tuple-element.42.rf_ref, f32[64,512]{1,0:T(8,128)S(1)} %coupling.1.refs_0_), custom_call_target="tpu_custom_call" | custom-call | flops 318767104 | bytes 4980736 | tf_op jit(solution)/shard_map/own_part/pallas_call | solution.py:289
  26.7 0.4 %collective-permute-done.7 = f32[64,512]{1,0:T(8,128)S(1)} collective-permute-done((f32[64,512]{1,0:T(8,128)S(1)}, f32[64,512]{1,0:T(8,128)S(1)}, u32[]{:S(2)}, u32[]{:S(2)}) %collective-permute-start.7) | collective-permute-done | bytes 131104 | tf_op jit(solution)/shard_map/ppermute | solution.py:311
  27.1 0.7 %add_bitcast_fusion = f32[1,512,64]{1,2,0:T(8,128)} fusion(f32[64,512]{1,0:T(8,128)S(1)} %own_part.1, f32[64,512]{1,0:T(8,128)S(1)} %collective-permute-done.7), kind=kLoop, calls=%fused_computation | loop fusion | flops 32768 | bytes 393216 | tf_op jit(solution)/shard_map/broadcast_in_dim | solution.py:440
  (5 shorter events, 0.1 us)
Async XLA Ops:
  0.0 2.8 %collective-permute-start = (bf16[64,512]{1,0:T(8,128)(2,1)}, bf16[64,512]{1,0:T(8,128)(2,1)S(1)}, u32[]{:S(2)}, u32[]{:S(2)}) collective-permute-start(bf16[64,512]{1,0:T(8,128)(2,1)} %bitcast.8), channel_id=1, source_target_pairs={{1,0},{0,1},{3,2},{2,3},{5,4},{4,5},{7,6},{6,7},{9,8},{8,9},{11,10... | collective-permute-start | bytes 196616 | tf_op jit(solution)/shard_map/ppermute | solution.py:311
  2.8 9.5 %copy-start = (s32[1,512]{1,0:T(1,128)S(1)}, s32[1,512]{1,0:T(1,128)}, u32[]{:S(2)}) copy-start(s32[1,512]{1,0:T(1,128)} %refs_2_.1) | copy-start | bytes 6148
  8.1 8.1 %collective-permute-start.3 = (f32[2,2432]{1,0:T(2,128)S(1)}, f32[2,2432]{1,0:T(2,128)S(1)}, u32[]{:S(2)}, u32[]{:S(2)}) collective-permute-start(f32[2,2432]{1,0:T(2,128)S(1)} %get-tuple-element.29.mean_ref), channel_id=1, source_target_pairs={{0,6},{2,4},{4,2},{6,0},{8,14},{10,12},{12,10},{14,8},{16,22},{18,... | collective-permute-start | bytes 58376 | tf_op jit(solution)/shard_map/ppermute | solution.py:332
  11.6 4.6 %collective-permute-start.2 = (f32[2,2432]{1,0:T(2,128)S(1)}, f32[2,2432]{1,0:T(2,128)S(1)}, u32[]{:S(2)}, u32[]{:S(2)}) collective-permute-start(f32[2,2432]{1,0:T(2,128)S(1)} %get-tuple-element.29.mean_ref), channel_id=1, source_target_pairs={{0,4},{2,6},{4,0},{6,2},{8,12},{10,14},{12,8},{14,10},{16,20},{18,... | collective-permute-start | bytes 58376 | tf_op jit(solution)/shard_map/ppermute | solution.py:332
  12.1 4.1 %collective-permute-start.1 = (f32[2,2432]{1,0:T(2,128)S(1)}, f32[2,2432]{1,0:T(2,128)S(1)}, u32[]{:S(2)}, u32[]{:S(2)}) collective-permute-start(f32[2,2432]{1,0:T(2,128)S(1)} %get-tuple-element.29.mean_ref), channel_id=1, source_target_pairs={{0,2},{2,0},{4,6},{6,4},{8,10},{10,8},{12,14},{14,12},{16,18},{18,... | collective-permute-start | bytes 58376 | tf_op jit(solution)/shard_map/ppermute | solution.py:332
  12.3 6.4 %collective-permute-start.5 = (s32[1,512]{1,0:T(1,128)S(1)}, s32[1,512]{1,0:T(1,128)S(1)}, u32[]{:S(2)}, u32[]{:S(2)}) collective-permute-start(s32[1,512]{1,0:T(1,128)S(1)} %copy-done), channel_id=1, source_target_pairs={{1,0},{0,1},{3,2},{2,3},{5,4},{4,5},{7,6},{6,7},{9,8},{8,9},{11,10... | collective-permute-start | bytes 6152 | tf_op jit(solution)/shard_map/ppermute | solution.py:311
  16.3 4.0 %collective-permute-start.4 = (f32[2,2432]{1,0:T(2,128)S(1)}, f32[2,2432]{1,0:T(2,128)S(1)}, u32[]{:S(2)}, u32[]{:S(2)}) collective-permute-start(f32[2,2432]{1,0:T(2,128)S(1)} %add_add_fusion), channel_id=1, source_target_pairs={{0,8},{2,10},{4,12},{6,14},{8,0},{10,2},{12,4},{14,6},{16,24},{18,... | collective-permute-start | bytes 58376 | tf_op jit(solution)/shard_map/ppermute | solution.py:332
  20.2 4.7 %collective-permute-start.6 = (f32[2,2432]{1,0:T(2,128)S(1)}, f32[2,2432]{1,0:T(2,128)S(1)}, u32[]{:S(2)}, u32[]{:S(2)}) collective-permute-start(f32[2,2432]{1,0:T(2,128)S(1)} %add.21), channel_id=1, source_target_pairs={{0,16},{2,18},{4,20},{6,22},{8,24},{10,26},{12,28},{14,30},{16,0},... | collective-permute-start | bytes 58376 | tf_op jit(solution)/shard_map/ppermute | solution.py:332
  25.6 1.5 %collective-permute-start.7 = (f32[64,512]{1,0:T(8,128)S(1)}, f32[64,512]{1,0:T(8,128)S(1)}, u32[]{:S(2)}, u32[]{:S(2)}) collective-permute-start(f32[64,512]{1,0:T(8,128)S(1)} %get-tuple-element.44), channel_id=1, source_target_pairs={{1,0},{0,1},{3,2},{2,3},{5,4},{4,5},{7,6},{6,7},{9,8},{8,9},{11,10... | collective-permute-start | bytes 393224 | tf_op jit(solution)/shard_map/ppermute | solution.py:311
